TPU v7x, 768 devices: a whole 4x8x12 slice. The times are simulated.
768 devices in a mesh: gx: 24 (over z_lo, x, core), gy: 32 (over y, z_hi).
Axes of the slice: x: 4, y: 8, z: 12 (z_hi: 4, z_lo: 3; z = z_hi * 3 + z_lo), core: 2. Of those that a mesh axis runs over, the one named last changes fastest.
Arguments:
- precursor: float32 [3, 96, 1024, 128], P(None, 'gx', 'gy'), may hold values from -6 to 6
- u_star: float32 [768, 1024, 128], P('gx', 'gy'), may hold values from -6 to 6
- v_star: float32 [768, 1024, 128], P('gx', 'gy'), may hold values from -6 to 6
- w_star: float32 [768, 1024, 128], P('gx', 'gy'), may hold values from -6 to 6
- heights: int32 [768, 1024], P('gx', 'gy'), may hold values from 0 to 41
Outputs:
- precursor_next: float32 [3, 96, 1024, 128], P(None, 'gx', 'gy')
- pressure: float32 [2, 128, 768, 1024], P(None, 'gy', 'gx')
Inputs may be any that keep to these rules, and one draw needn't show every extreme that they name: `heights`: cells of a column at levels below its height are solid.
All inputs are finite; a program needn't handle non-finite values.
Results may differ from a plain program's by a relative error of at most 0.00011.
Values sent between devices are 32-bit elements; how exact they have to be, the bound alone decides.
A program may use at most 32 MiB of HBM per device.

v0:
```python
import math

import jax
import jax.numpy as jnp
from jax import lax
from jax.sharding import PartitionSpec as P

ITERS = 4


step_size = 0.1
viscosity = 0.2
highest = lax.Precision.HIGHEST


def padded_2(block, sides, width, periodic):
    for axis, dim in sides:
        count = lax.axis_size(axis)
        forward = [(i, i + 1) for i in range(count - 1)]
        if periodic:
            forward.append((count - 1, 0))
        backward = [(target, source) for source, target in forward]
        low = lax.ppermute(
            lax.slice_in_dim(block, block.shape[dim] - width, None, axis=dim), axis, forward
        )
        high = lax.ppermute(lax.slice_in_dim(block, 0, width, axis=dim), axis, backward)
        block = jnp.concatenate([low, block, high], axis=dim)
    return block


def from_behind(value, axis, steps):
    count = lax.axis_size(axis)
    pairs = [(source, (source + steps) % count) for source in range(count)]
    return lax.ppermute(value, axis, pairs)


def vertical_table(levels):
    modes = lax.broadcasted_iota(jnp.int32, (levels, levels), 0)
    cells = lax.broadcasted_iota(jnp.int32, (levels, levels), 1)
    phase = modes * (2 * cells + 1) % (4 * levels)
    weight = jnp.where(modes == 0, 1.0, 2.0).astype(jnp.float32) / levels
    return jnp.sqrt(weight) * jnp.cos(phase.astype(jnp.float32) * (math.pi / (2 * levels)))


def span_tables(width):
    rows = lax.broadcasted_iota(jnp.int32, (width, width), 0)
    cols = lax.broadcasted_iota(jnp.int32, (width, width), 1)
    angle = (rows * cols % width).astype(jnp.float32) * (2.0 * math.pi / width)
    scale = 1.0 / math.sqrt(width)
    return (jnp.cos(angle) * scale, jnp.sin(angle) * scale)


def precursor_section(padded):
    center = padded[:, 1:-1, 1:-1]
    east = padded[:, 2:, 1:-1]
    west = padded[:, :-2, 1:-1]
    north = padded[:, 1:-1, 2:]
    south = padded[:, 1:-1, :-2]
    lifted = jnp.pad(center, ((0, 0), (0, 0), (0, 0), (1, 1)))
    above = lifted[..., 2:]
    below = lifted[..., :-2]
    advect = (
        center[0:1] * (east - west) * 0.5
        + center[1:2] * (north - south) * 0.5
        + center[2:3] * (above - below) * 0.5
    )
    spread = east + west + north + south + above + below - 6.0 * center
    return center + step_size * (viscosity * spread - advect)


def sweep(rhs_both, extended, diagonal):
    return (rhs_both + extended[:, :, :-2] + extended[:, :, 2:]) / diagonal


def on_device(precursor, u_star, v_star, w_star, heights):
    padded = padded_2(precursor, (("gx", 1), ("gy", 2)), 1, True)
    precursor_next = precursor_section(padded)
    levels = lax.broadcasted_iota(jnp.int32, u_star.shape, 2)
    open_cells = (levels >= heights[:, :, None]).astype(jnp.float32)
    u_open = u_star * open_cells
    v_open = v_star * open_cells
    w_open = w_star * open_cells
    is_last = lax.axis_index("gx") == lax.axis_size("gx") - 1
    outgoing = jnp.where(is_last, precursor_next[0, -1], u_open[-1])
    first_plane = from_behind(outgoing, "gx", 1)
    u_prev = jnp.concatenate([first_plane[None], u_open[:-1]], 0)
    w_prev = jnp.concatenate([jnp.zeros_like(w_open[:, :, :1]), w_open[:, :, :-1]], 2)
    level_count = u_star.shape[2]
    table = vertical_table(level_count)
    span_width = u_star.shape[1] * lax.axis_size("gy")
    cos_table, sin_table = span_tables(span_width)
    span_edge = from_behind(v_open[:, -1], "gy", 1)
    v_prev = jnp.concatenate([span_edge[:, None], v_open[:, :-1]], 1)
    rhs = -(u_open - u_prev + (v_open - v_prev) + (w_open - w_prev))
    columns = lax.all_to_all(
        jnp.einsum("mk,xyk->mxy", table, rhs, precision=highest),
        "gy",
        split_axis=0,
        concat_axis=2,
        tiled=True,
    )
    flat = columns.reshape(-1, span_width)
    real_part = jnp.dot(flat, cos_table, precision=highest).reshape(columns.shape)
    imag_part = -jnp.dot(flat, sin_table, precision=highest).reshape(columns.shape)
    rhs_both = jnp.stack([real_part, imag_part])
    mode_count = rhs_both.shape[1]
    modes = (
        lax.axis_index("gy") * mode_count + lax.broadcasted_iota(jnp.int32, (mode_count, 1, 1), 0)
    ).astype(jnp.float32)
    waves = lax.broadcasted_iota(jnp.int32, (1, 1, span_width), 2).astype(jnp.float32)
    diagonal = (
        6.0
        - 2.0 * jnp.cos(modes * (math.pi / level_count))
        - 2.0 * jnp.cos(waves * (2.0 * math.pi / span_width))
    )
    pressure = jnp.zeros_like(rhs_both)
    for turn in range(ITERS):
        extended = padded_2(pressure, (("gx", 2),), 1, False)
        pressure = sweep(rhs_both, extended, diagonal)
    return (precursor_next, pressure)


def solution(mesh):
    placed = (
        P(None, "gx", "gy", None),
        P("gx", "gy", None),
        P("gx", "gy", None),
        P("gx", "gy", None),
        P("gx", "gy"),
    )
    return jax.shard_map(
        on_device,
        mesh=mesh,
        in_specs=placed,
        out_specs=(P(None, "gx", "gy", None), P(None, "gy", "gx", None)),
        check_vma=False,
    )
```

profile of v0, /device:TPU:79, one launch (start us, length us, event | category | flops | bytes accessed | tf_op | source)
XLA Modules:
  0.0 158.5 jit_solution(72170122979325296)
XLA Ops:
  0.6 0.0 copy-start
  0.6 0.9 fusion.94
  1.5 4.5 %collective-permute-start.1 = (f32[3,1,32,128]{3,2,1,0:T(8,128)S(1)}, f32[3,1,32,128]{3,2,1,0:T(8,128)S(1)}, u32[]{:S(2)}, u32[]{:S(2)}) collective-permute-start(f32[3,1,32,128]{3,2,1,0:T(8,128)S(1)} %get-tuple-element.14), channel_id=1, source_target_pairs={{0,32},{32,64},{64,96},{96,128},{128,160},{160,192},{192,224},{224... | collective-permute-start | bytes 147464 | tf_op jit(solution)/shard_map/ppermute | solution.py:23
  6.0 1.9 %collective-permute-start = (f32[3,1,32,128]{3,2,1,0:T(8,128)S(1)}, f32[3,1,32,128]{3,2,1,0:T(8,128)S(1)}, u32[]{:S(2)}, u32[]{:S(2)}) collective-permute-start(f32[3,1,32,128]{3,2,1,0:T(8,128)S(1)} %get-tuple-element.13), channel_id=1, source_target_pairs={{32,0},{64,32},{96,64},{128,96},{160,128},{192,160},{224,192},{256... | collective-permute-start | bytes 147464 | tf_op jit(solution)/shard_map/ppermute | solution.py:26
  7.9 1.6 %fusion.50 = (f32[32,32,128]{2,1,0:T(8,128)S(1)}, f32[32,32,128]{2,1,0:T(8,128)S(1)}, f32[32,32,128]{2,1,0:T(8,128)S(1)}) fusion(f32[32,32,128]{2,1,0:T(8,128)} %param.8, s32[32,32]{1,0:T(8,128)} %param.9, f32[32,32,128]{2,1,0:T(8,128)} %param.7, f32[32,32,128]{2,1,0:T(8,128)} %param.6), kind=kLoop, calls=%fused_computation.56 | loop fusion | flops 524288 | bytes 3149824 | tf_op jit(solution)/shard_map/mul | solution.py:82
  9.6 8.8 %collective-permute-start.5 = (f32[32,128]{1,0:T(8,128)S(1)}, f32[32,128]{1,0:T(8,128)S(1)}, u32[]{:S(2)}, u32[]{:S(2)}) collective-permute-start(f32[32,128]{1,0:T(8,128)S(1)} %bitcast.52), channel_id=1, source_target_pairs={{0,1},{1,2},{2,3},{3,4},{4,5},{5,6},{6,7},{7,8},{8,9},{9,10},{10,1... | collective-permute-start | bytes 49160 | tf_op jit(solution)/shard_map/ppermute | solution.py:34
  18.4 0.0 copy-done
  18.5 0.0 collective-permute-done.1
  18.5 0.0 collective-permute-done
  18.6 7.3 %collective-permute-start.2 = (f32[3,6,1,128]{3,2,1,0:T(1,128)S(1)}, f32[3,6,1,128]{3,2,1,0:T(1,128)S(1)}, u32[]{:S(2)}, u32[]{:S(2)}) collective-permute-start(f32[3,6,1,128]{3,2,1,0:T(1,128)S(1)} %get-tuple-element.8), channel_id=1, source_target_pairs={{1,0},{2,1},{3,2},{4,3},{5,4},{6,5},{7,6},{8,7},{9,8},{10,9},{11,1... | collective-permute-start | bytes 27656 | tf_op jit(solution)/shard_map/ppermute | solution.py:26
  25.9 1.9 %collective-permute-start.3 = (f32[3,6,1,128]{3,2,1,0:T(1,128)S(1)}, f32[3,6,1,128]{3,2,1,0:T(1,128)S(1)}, u32[]{:S(2)}, u32[]{:S(2)}) collective-permute-start(f32[3,6,1,128]{3,2,1,0:T(1,128)S(1)} %get-tuple-element.9), channel_id=1, source_target_pairs={{0,1},{1,2},{2,3},{3,4},{4,5},{5,6},{6,7},{7,8},{8,9},{9,10},{10,1... | collective-permute-start | bytes 27656 | tf_op jit(solution)/shard_map/ppermute | solution.py:23
  27.9 0.0 collective-permute-done.2
  27.9 6.4 %collective-permute-done.3 = f32[3,6,1,128]{3,2,1,0:T(1,128)S(1)} collective-permute-done((f32[3,6,1,128]{3,2,1,0:T(1,128)S(1)}, f32[3,6,1,128]{3,2,1,0:T(1,128)S(1)}, u32[]{:S(2)}, u32[]{:S(2)}) %collective-permute-start.3) | collective-permute-done | bytes 9248 | tf_op jit(solution)/shard_map/ppermute | solution.py:23
  34.3 0.2 multiply_add_fusion
  34.5 0.0 copy-start.1
  34.5 5.3 %collective-permute-start.4 = (f32[32,128]{1,0:T(8,128)S(1)}, f32[32,128]{1,0:T(8,128)S(1)}, u32[]{:S(2)}, u32[]{:S(2)}) collective-permute-start(f32[32,128]{1,0:T(8,128)S(1)} %fusion.71), channel_id=1, source_target_pairs={{0,32},{32,64},{64,96},{96,128},{128,160},{160,192},{192,224},{224... | collective-permute-start | bytes 49160 | tf_op jit(solution)/shard_map/ppermute | solution.py:34
  39.9 0.0 collective-permute-done.5
  39.9 0.8 collective-permute-done.4
  40.7 0.9 fusion.42
  41.6 0.0 copy-done.1
  41.6 1.8 %copy.13 = f32[128,32,32]{2,1,0:T(8,128)S(1)} copy(f32[128,32,32]{0,2,1:T(8,128)S(1)} %fusion.42) | data formatting | bytes 1048576 | tf_op jit(solution)/shard_map/mk,xyk->mxy/dot_general | solution.py:96
  43.5 1.7 %reshape.81 = f32[32,1,4096]{2,1,0:T(1,128)} reshape(f32[128,32,32]{2,1,0:T(8,128)S(1)} %copy.13) | data formatting | bytes 1048576
  45.2 12.5 %all-to-all-start = ((f32[32,1,4096]{2,1,0:T(1,128)}), f32[32,1,4096]{2,1,0:T(1,128)S(1)}, u32[]{:S(2)}, u32[]{:S(2)}) async-start(f32[32,1,4096]{2,1,0:T(1,128)} %reshape.81), calls=%async_computation | async-start | bytes 1048576 | tf_op jit(solution)/shard_map/all_to_all | solution.py:95
  57.7 7.5 %collective-permute-start.6 = (f32[2,4,1,1024]{3,2,1,0:T(1,128)S(1)}, f32[2,4,1,1024]{3,2,1,0:T(1,128)S(1)}, u32[]{:S(2)}, u32[]{:S(2)}) collective-permute-start(f32[2,4,1,1024]{3,2,1,0:T(1,128)S(1)} %broadcast.112), channel_id=1, source_target_pairs={{0,32},{32,64},{64,96},{96,128},{128,160},{160,192},{192,224},{224... | collective-permute-start | bytes 98312 | tf_op jit(solution)/shard_map/ppermute | solution.py:23
  65.2 1.9 %collective-permute-start.7 = (f32[2,4,1,1024]{3,2,1,0:T(1,128)S(1)}, f32[2,4,1,1024]{3,2,1,0:T(1,128)S(1)}, u32[]{:S(2)}, u32[]{:S(2)}) collective-permute-start(f32[2,4,1,1024]{3,2,1,0:T(1,128)S(1)} %broadcast.112), channel_id=1, source_target_pairs={{32,0},{64,32},{96,64},{128,96},{160,128},{192,160},{224,192},{256... | collective-permute-start | bytes 98312 | tf_op jit(solution)/shard_map/ppermute | solution.py:26
  67.2 0.1 broadcast_subtract_fusion
  67.3 16.1 %all-to-all-done = f32[32,1,4096]{2,1,0:T(1,128)S(1)} async-done(((f32[32,1,4096]{2,1,0:T(1,128)}), f32[32,1,4096]{2,1,0:T(1,128)S(1)}, u32[]{:S(2)}, u32[]{:S(2)}) %all-to-all-start) | async-done | bytes 524320 | tf_op jit(solution)/shard_map/all_to_all | solution.py:95
  83.4 0.5 broadcast.154
  83.9 1.9 %reduce = f32[32,4096]{1,0:T(8,128)S(1)} reduce(f32[32,1,4096]{2,1,0:T(1,128)S(1)} %all-to-all-done, f32[]{:T(128)} %broadcast.154), dimensions={1}, to_apply=%all_to_all.11.reduce_sub_computation | reduce | bytes 1048580 | tf_op jit(solution)/shard_map/all_to_all | solution.py:95
  85.8 0.7 reshape.82
  86.5 2.6 %copy.14 = f32[4,32,32,32]{3,2,1,0:T(8,128)} copy(f32[4,32,32,32]{3,1,0,2:T(8,128)S(1)} %bitcast.47) | data formatting | bytes 1048576 | tf_op jit(solution)/shard_map/all_to_all | solution.py:95
  89.0 2.4 %reshape.77 = f32[4,32,1024]{2,1,0:T(8,128)S(1)} reshape(f32[4,32,32,32]{3,2,1,0:T(8,128)} %copy.14) | data formatting | bytes 1048576 | tf_op jit(solution)/shard_map/reshape.32
  91.5 18.4 %fusion.24 = f32[1,4,32,1024]{3,2,1,0:T(8,128)S(1)} fusion(f32[4,32,1024]{2,1,0:T(8,128)S(1)} %reshape.77), kind=kOutput, calls=%fused_computation.23 | convolution fusion | flops 1626472448 | bytes 1048576 | tf_op jit(solution)/shard_map/dot_general | solution.py:104
  109.9 18.4 %fusion.18 = f32[1,4,32,1024]{3,2,1,0:T(8,128)S(1)} fusion(f32[4,32,1024]{2,1,0:T(8,128)S(1)} %reshape.77), kind=kOutput, calls=%fused_computation.21 | convolution fusion | flops 1626341376 | bytes 1048576 | tf_op jit(solution)/shard_map/dot_general | solution.py:103
  128.3 0.0 collective-permute-done.6
  128.3 0.0 collective-permute-done.7
  128.3 0.2 fusion.29
  128.5 0.1 fusion.92
  128.6 1.9 %collective-permute-start.8 = (f32[2,4,1,1024]{3,2,1,0:T(1,128)S(1)}, f32[2,4,1,1024]{3,2,1,0:T(1,128)S(1)}, u32[]{:S(2)}, u32[]{:S(2)}) collective-permute-start(f32[2,4,1,1024]{3,2,1,0:T(1,128)S(1)} %get-tuple-element.6), channel_id=1, source_target_pairs={{0,32},{32,64},{64,96},{96,128},{128,160},{160,192},{192,224},{224... | collective-permute-start | bytes 98312 | tf_op jit(solution)/shard_map/ppermute | solution.py:23
  130.5 2.4 %collective-permute-start.9 = (f32[2,4,1,1024]{3,2,1,0:T(1,128)S(1)}, f32[2,4,1,1024]{3,2,1,0:T(1,128)S(1)}, u32[]{:S(2)}, u32[]{:S(2)}) collective-permute-start(f32[2,4,1,1024]{3,2,1,0:T(1,128)S(1)} %get-tuple-element.7), channel_id=1, source_target_pairs={{32,0},{64,32},{96,64},{128,96},{160,128},{192,160},{224,192},{256... | collective-permute-start | bytes 98312 | tf_op jit(solution)/shard_map/ppermute | solution.py:26
  132.9 0.0 collective-permute-done.8
  132.9 4.9 %collective-permute-done.9 = f32[2,4,1,1024]{3,2,1,0:T(1,128)S(1)} collective-permute-done((f32[2,4,1,1024]{3,2,1,0:T(1,128)S(1)}, f32[2,4,1,1024]{3,2,1,0:T(1,128)S(1)}, u32[]{:S(2)}, u32[]{:S(2)}) %collective-permute-start.9) | collective-permute-done | bytes 32800 | tf_op jit(solution)/shard_map/ppermute | solution.py:26
  137.8 0.4 fusion.37
  138.2 0.1 fusion.91
  138.2 1.9 %collective-permute-start.10 = (f32[2,4,1,1024]{3,2,1,0:T(1,128)S(1)}, f32[2,4,1,1024]{3,2,1,0:T(1,128)S(1)}, u32[]{:S(2)}, u32[]{:S(2)}) collective-permute-start(f32[2,4,1,1024]{3,2,1,0:T(1,128)S(1)} %get-tuple-element.4), channel_id=1, source_target_pairs={{0,32},{32,64},{64,96},{96,128},{128,160},{160,192},{192,224},{224... | collective-permute-start | bytes 98312 | tf_op jit(solution)/shard_map/ppermute | solution.py:23
  140.2 2.4 %collective-permute-start.11 = (f32[2,4,1,1024]{3,2,1,0:T(1,128)S(1)}, f32[2,4,1,1024]{3,2,1,0:T(1,128)S(1)}, u32[]{:S(2)}, u32[]{:S(2)}) collective-permute-start(f32[2,4,1,1024]{3,2,1,0:T(1,128)S(1)} %get-tuple-element.5), channel_id=1, source_target_pairs={{32,0},{64,32},{96,64},{128,96},{160,128},{192,160},{224,192},{256... | collective-permute-start | bytes 98312 | tf_op jit(solution)/shard_map/ppermute | solution.py:26
  142.6 0.0 collective-permute-done.10
  142.6 4.9 %collective-permute-done.11 = f32[2,4,1,1024]{3,2,1,0:T(1,128)S(1)} collective-permute-done((f32[2,4,1,1024]{3,2,1,0:T(1,128)S(1)}, f32[2,4,1,1024]{3,2,1,0:T(1,128)S(1)}, u32[]{:S(2)}, u32[]{:S(2)}) %collective-permute-start.11) | collective-permute-done | bytes 32800 | tf_op jit(solution)/shard_map/ppermute | solution.py:26
  147.5 0.4 fusion.34
  147.9 0.1 fusion.90
  147.9 1.9 %collective-permute-start.12 = (f32[2,4,1,1024]{3,2,1,0:T(1,128)S(1)}, f32[2,4,1,1024]{3,2,1,0:T(1,128)S(1)}, u32[]{:S(2)}, u32[]{:S(2)}) collective-permute-start(f32[2,4,1,1024]{3,2,1,0:T(1,128)S(1)} %get-tuple-element.2), channel_id=1, source_target_pairs={{0,32},{32,64},{64,96},{96,128},{128,160},{160,192},{192,224},{224... | collective-permute-start | bytes 98312 | tf_op jit(solution)/shard_map/ppermute | solution.py:23
  149.9 2.4 %collective-permute-start.13 = (f32[2,4,1,1024]{3,2,1,0:T(1,128)S(1)}, f32[2,4,1,1024]{3,2,1,0:T(1,128)S(1)}, u32[]{:S(2)}, u32[]{:S(2)}) collective-permute-start(f32[2,4,1,1024]{3,2,1,0:T(1,128)S(1)} %get-tuple-element.3), channel_id=1, source_target_pairs={{32,0},{64,32},{96,64},{128,96},{160,128},{192,160},{224,192},{256... | collective-permute-start | bytes 98312 | tf_op jit(solution)/shard_map/ppermute | solution.py:26
  152.3 0.0 collective-permute-done.12
  152.3 4.9 %collective-permute-done.13 = f32[2,4,1,1024]{3,2,1,0:T(1,128)S(1)} collective-permute-done((f32[2,4,1,1024]{3,2,1,0:T(1,128)S(1)}, f32[2,4,1,1024]{3,2,1,0:T(1,128)S(1)}, u32[]{:S(2)}, u32[]{:S(2)}) %collective-permute-start.13) | collective-permute-done | bytes 32800 | tf_op jit(solution)/shard_map/ppermute | solution.py:26
  157.2 1.3 fusion.31
  (13 shorter events, 0.2 us)
Async XLA Ops:
  0.6 17.8 %copy-start = (f32[3,4,32,128]{3,2,1,0:T(8,128)S(1)}, f32[3,4,32,128]{3,2,1,0:T(8,128)}, u32[]{:S(2)}) copy-start(f32[3,4,32,128]{3,2,1,0:T(8,128)} %param.5) | copy-start | bytes 589828
  1.5 17.0 %collective-permute-start.1 = (f32[3,1,32,128]{3,2,1,0:T(8,128)S(1)}, f32[3,1,32,128]{3,2,1,0:T(8,128)S(1)}, u32[]{:S(2)}, u32[]{:S(2)}) collective-permute-start(f32[3,1,32,128]{3,2,1,0:T(8,128)S(1)} %get-tuple-element.14), channel_id=1, source_target_pairs={{0,32},{32,64},{64,96},{96,128},{128,160},{160,192},{192,224},{224... | collective-permute-start | bytes 147464 | tf_op jit(solution)/shard_map/ppermute | solution.py:23
  6.0 12.5 %collective-permute-start = (f32[3,1,32,128]{3,2,1,0:T(8,128)S(1)}, f32[3,1,32,128]{3,2,1,0:T(8,128)S(1)}, u32[]{:S(2)}, u32[]{:S(2)}) collective-permute-start(f32[3,1,32,128]{3,2,1,0:T(8,128)S(1)} %get-tuple-element.13), channel_id=1, source_target_pairs={{32,0},{64,32},{96,64},{128,96},{160,128},{192,160},{224,192},{256... | collective-permute-start | bytes 147464 | tf_op jit(solution)/shard_map/ppermute | solution.py:26
  9.6 30.3 %collective-permute-start.5 = (f32[32,128]{1,0:T(8,128)S(1)}, f32[32,128]{1,0:T(8,128)S(1)}, u32[]{:S(2)}, u32[]{:S(2)}) collective-permute-start(f32[32,128]{1,0:T(8,128)S(1)} %bitcast.52), channel_id=1, source_target_pairs={{0,1},{1,2},{2,3},{3,4},{4,5},{5,6},{6,7},{7,8},{8,9},{9,10},{10,1... | collective-permute-start | bytes 49160 | tf_op jit(solution)/shard_map/ppermute | solution.py:34
  18.6 9.3 %collective-permute-start.2 = (f32[3,6,1,128]{3,2,1,0:T(1,128)S(1)}, f32[3,6,1,128]{3,2,1,0:T(1,128)S(1)}, u32[]{:S(2)}, u32[]{:S(2)}) collective-permute-start(f32[3,6,1,128]{3,2,1,0:T(1,128)S(1)} %get-tuple-element.8), channel_id=1, source_target_pairs={{1,0},{2,1},{3,2},{4,3},{5,4},{6,5},{7,6},{8,7},{9,8},{10,9},{11,1... | collective-permute-start | bytes 27656 | tf_op jit(solution)/shard_map/ppermute | solution.py:26
  25.9 8.4 %collective-permute-start.3 = (f32[3,6,1,128]{3,2,1,0:T(1,128)S(1)}, f32[3,6,1,128]{3,2,1,0:T(1,128)S(1)}, u32[]{:S(2)}, u32[]{:S(2)}) collective-permute-start(f32[3,6,1,128]{3,2,1,0:T(1,128)S(1)} %get-tuple-element.9), channel_id=1, source_target_pairs={{0,1},{1,2},{2,3},{3,4},{4,5},{5,6},{6,7},{7,8},{8,9},{9,10},{10,1... | collective-permute-start | bytes 27656 | tf_op jit(solution)/shard_map/ppermute | solution.py:23
  34.5 7.1 %copy-start.1 = (f32[3,4,32,128]{3,2,1,0:T(8,128)}, f32[3,4,32,128]{3,2,1,0:T(8,128)S(1)}, u32[]{:S(2)}) copy-start(f32[3,4,32,128]{3,2,1,0:T(8,128)S(1)} %multiply_add_fusion) | copy-start | bytes 589828
  34.5 6.2 %collective-permute-start.4 = (f32[32,128]{1,0:T(8,128)S(1)}, f32[32,128]{1,0:T(8,128)S(1)}, u32[]{:S(2)}, u32[]{:S(2)}) collective-permute-start(f32[32,128]{1,0:T(8,128)S(1)} %fusion.71), channel_id=1, source_target_pairs={{0,32},{32,64},{64,96},{96,128},{128,160},{160,192},{192,224},{224... | collective-permute-start | bytes 49160 | tf_op jit(solution)/shard_map/ppermute | solution.py:34
  45.2 38.2 %all-to-all-start = ((f32[32,1,4096]{2,1,0:T(1,128)}), f32[32,1,4096]{2,1,0:T(1,128)S(1)}, u32[]{:S(2)}, u32[]{:S(2)}) async-start(f32[32,1,4096]{2,1,0:T(1,128)} %reshape.81), calls=%async_computation | async-start | bytes 1048576 | tf_op jit(solution)/shard_map/all_to_all | solution.py:95
  57.7 70.5 %collective-permute-start.6 = (f32[2,4,1,1024]{3,2,1,0:T(1,128)S(1)}, f32[2,4,1,1024]{3,2,1,0:T(1,128)S(1)}, u32[]{:S(2)}, u32[]{:S(2)}) collective-permute-start(f32[2,4,1,1024]{3,2,1,0:T(1,128)S(1)} %broadcast.112), channel_id=1, source_target_pairs={{0,32},{32,64},{64,96},{96,128},{128,160},{160,192},{192,224},{224... | collective-permute-start | bytes 98312 | tf_op jit(solution)/shard_map/ppermute | solution.py:23
  65.2 63.1 %collective-permute-start.7 = (f32[2,4,1,1024]{3,2,1,0:T(1,128)S(1)}, f32[2,4,1,1024]{3,2,1,0:T(1,128)S(1)}, u32[]{:S(2)}, u32[]{:S(2)}) collective-permute-start(f32[2,4,1,1024]{3,2,1,0:T(1,128)S(1)} %broadcast.112), channel_id=1, source_target_pairs={{32,0},{64,32},{96,64},{128,96},{160,128},{192,160},{224,192},{256... | collective-permute-start | bytes 98312 | tf_op jit(solution)/shard_map/ppermute | solution.py:26
  128.6 4.3 %collective-permute-start.8 = (f32[2,4,1,1024]{3,2,1,0:T(1,128)S(1)}, f32[2,4,1,1024]{3,2,1,0:T(1,128)S(1)}, u32[]{:S(2)}, u32[]{:S(2)}) collective-permute-start(f32[2,4,1,1024]{3,2,1,0:T(1,128)S(1)} %get-tuple-element.6), channel_id=1, source_target_pairs={{0,32},{32,64},{64,96},{96,128},{128,160},{160,192},{192,224},{224... | collective-permute-start | bytes 98312 | tf_op jit(solution)/shard_map/ppermute | solution.py:23
  130.5 7.3 %collective-permute-start.9 = (f32[2,4,1,1024]{3,2,1,0:T(1,128)S(1)}, f32[2,4,1,1024]{3,2,1,0:T(1,128)S(1)}, u32[]{:S(2)}, u32[]{:S(2)}) collective-permute-start(f32[2,4,1,1024]{3,2,1,0:T(1,128)S(1)} %get-tuple-element.7), channel_id=1, source_target_pairs={{32,0},{64,32},{96,64},{128,96},{160,128},{192,160},{224,192},{256... | collective-permute-start | bytes 98312 | tf_op jit(solution)/shard_map/ppermute | solution.py:26
  138.2 4.3 %collective-permute-start.10 = (f32[2,4,1,1024]{3,2,1,0:T(1,128)S(1)}, f32[2,4,1,1024]{3,2,1,0:T(1,128)S(1)}, u32[]{:S(2)}, u32[]{:S(2)}) collective-permute-start(f32[2,4,1,1024]{3,2,1,0:T(1,128)S(1)} %get-tuple-element.4), channel_id=1, source_target_pairs={{0,32},{32,64},{64,96},{96,128},{128,160},{160,192},{192,224},{224... | collective-permute-start | bytes 98312 | tf_op jit(solution)/shard_map/ppermute | solution.py:23
  140.2 7.3 %collective-permute-start.11 = (f32[2,4,1,1024]{3,2,1,0:T(1,128)S(1)}, f32[2,4,1,1024]{3,2,1,0:T(1,128)S(1)}, u32[]{:S(2)}, u32[]{:S(2)}) collective-permute-start(f32[2,4,1,1024]{3,2,1,0:T(1,128)S(1)} %get-tuple-element.5), channel_id=1, source_target_pairs={{32,0},{64,32},{96,64},{128,96},{160,128},{192,160},{224,192},{256... | collective-permute-start | bytes 98312 | tf_op jit(solution)/shard_map/ppermute | solution.py:26
  147.9 4.3 %collective-permute-start.12 = (f32[2,4,1,1024]{3,2,1,0:T(1,128)S(1)}, f32[2,4,1,1024]{3,2,1,0:T(1,128)S(1)}, u32[]{:S(2)}, u32[]{:S(2)}) collective-permute-start(f32[2,4,1,1024]{3,2,1,0:T(1,128)S(1)} %get-tuple-element.2), channel_id=1, source_target_pairs={{0,32},{32,64},{64,96},{96,128},{128,160},{160,192},{192,224},{224... | collective-permute-start | bytes 98312 | tf_op jit(solution)/shard_map/ppermute | solution.py:23
  149.9 7.3 %collective-permute-start.13 = (f32[2,4,1,1024]{3,2,1,0:T(1,128)S(1)}, f32[2,4,1,1024]{3,2,1,0:T(1,128)S(1)}, u32[]{:S(2)}, u32[]{:S(2)}) collective-permute-start(f32[2,4,1,1024]{3,2,1,0:T(1,128)S(1)} %get-tuple-element.3), channel_id=1, source_target_pairs={{32,0},{64,32},{96,64},{128,96},{160,128},{192,160},{224,192},{256... | collective-permute-start | bytes 98312 | tf_op jit(solution)/shard_map/ppermute | solution.py:26
where the time goes:
time: 159 us; the launch traced here: 158 us
  starting transfers between devices  64.7 us (41%)
  waiting for transfers between devices  38.1 us (24%)
  matrix products  37.7 us (24%)
  local copies, waits for them, and re-layouts  10.9 us (7%)
  other arithmetic  6.11 us (4%)
    ppermute x6, starting transfers between devices, padded_2(): lax.ppermute(lax.slice_in_dim(block, block.shape[dim] - width, None, axis...  19.6 us
    dot_general x1, matrix products, on_device(): jnp.dot(flat, sin_table, precision=highest).reshape(columns.shape)  18.4 us
    ppermute x6, starting transfers between devices, padded_2(): lax.ppermute(lax.slice_in_dim(block, 0, width, axis=dim), axis, backward)  18.4 us
    dot_general x1, matrix products, on_device(): jnp.dot(flat, cos_table, precision=highest).reshape(columns.shape)  18.4 us
    all_to_all x1, waiting for transfers between devices, on_device(): lax.all_to_all(jnp.einsum('mk,xyk->mxy', table, rhs, precision=highest),...  16.1 us
    ppermute x6, waiting for transfers between devices, padded_2(): lax.ppermute(lax.slice_in_dim(block, 0, width, axis=dim), axis, backward)  14.8 us
    ppermute x2, starting transfers between devices, from_behind(): return lax.ppermute(value, axis, pairs)  14.1 us
    all_to_all x1, starting transfers between devices, on_device(): lax.all_to_all(jnp.einsum('mk,xyk->mxy', table, rhs, precision=highest),...  12.5 us
  transfers between devices with their start and end apart: 15, of which 6 were waited for; matrix products, arithmetic and copies ran while one was open for 30% of the time, Pallas kernels for 0%

commit v1 on v0

v1 whole, which is shorter than its diff:
```python
import math

import jax
import jax.numpy as jnp
import numpy as np
from jax import lax
from jax.experimental import pallas as pl
from jax.experimental.pallas import tpu as pltpu
from jax.sharding import PartitionSpec as P

ITERS = 4
NY = 8
NZ = 4
MESH = pl.DeviceIdType.MESH
F32 = jnp.float32
BF16 = jnp.bfloat16
CHUNKS = ((0, 1, 2, 3, 12, 13, 14, 15), (4, 5, 6, 7, 8, 9, 10, 11))


def split(value):
    high = value.astype(BF16)
    return high, (value - high.astype(F32)).astype(BF16)


def vertical_tables(levels, groups):
    modes = np.arange(levels)[:, None]
    cells = np.arange(levels)[None, :]
    weight = np.where(modes == 0, 1.0, 2.0) / levels
    table = np.sqrt(weight) * np.cos(modes * (2 * cells + 1) % (4 * levels) * (math.pi / (2 * levels)))
    both = np.zeros((levels, 2, 2, levels))
    both[:, 0, 0] = table
    both[:, 1, 1] = table
    return both.reshape(2 * levels, 2 * levels).astype(np.float32)


def span_tables(width):
    half = width // 2
    y = np.arange(width)[:, None]
    cos = np.cos(y * np.arange(half + 1)[None] % width * (2 * math.pi / width))
    sin = np.sin(y * np.arange(1, half)[None] % width * (2 * math.pi / width))
    table = np.concatenate([cos, -sin], 1) / math.sqrt(width)
    cells = width // (NY * NZ)
    table = table.reshape(NY, NZ, cells, width).transpose(1, 0, 2, 3).reshape(NZ, NY * cells, width)
    return table.astype(np.float32)


def inverse_diagonal(levels, width, groups):
    modes = np.arange(levels).reshape(groups, levels // groups, 1, 1)
    half = width // 2
    waves = np.concatenate([np.arange(half + 1), np.arange(1, half)])
    diagonal = 6.0 - 2.0 * np.cos(modes * (math.pi / levels)) - 2.0 * np.cos(waves * (2 * math.pi / width))
    both = np.broadcast_to(1.0 / diagonal, (groups, levels // groups, 2, width))
    return both.reshape(groups, 2 * levels // groups, width).astype(np.float32)


def lane_shift(value, up):
    levels = value.shape[1]
    lane = lax.broadcasted_iota(jnp.int32, value.shape, 1)
    if up:
        return jnp.where(lane == levels - 1, 0.0, pltpu.roll(value, levels - 1, 1))
    return jnp.where(lane == 0, 0.0, pltpu.roll(value, 1, 1))


def row_shift(value, edge, up):
    count = value.shape[0]
    row = lax.broadcasted_iota(jnp.int32, value.shape, 0)
    if up:
        return jnp.where(row == count - 1, edge, pltpu.roll(value, count - 1, 0))
    return jnp.where(row == 0, edge, pltpu.roll(value, 1, 0))


def stencil(q, a, b, c, east, west, north, south):
    above = lane_shift(q, True)
    below = lane_shift(q, False)
    advect = a * (east - west) * 0.5 + b * (north - south) * 0.5 + c * (above - below) * 0.5
    spread = east + west + north + south + above + below - 6.0 * q
    return q + 0.1 * (0.2 * spread - advect)


def kernel(
    prec_hbm, u_hbm, v_hbm, w_hbm, heights_hbm, vert_hbm, span_hbm, inv_hbm,
    next_hbm, press_hbm,
    prec, u, v, w, heights, vert_f32, span_f32, inv, vert, span_hi, span_lo,
    u_out, south_out, north_out, u_in, south_in, north_in, west_in, east_in, corner_in, u_before,
    rhs, rhs_hi, rhs_lo, outgoing, incoming, bands, left_in, right_in, solved, next_v, press_v,
    load_sem, halo_send, halo_recv, send_sem, recv_sem, edge_send, edge_recv, store_sem,
):
    gx, gy = lax.axis_index("gx"), lax.axis_index("gy")
    count_x, count_y = lax.axis_size("gx"), lax.axis_size("gy")
    my_y, my_z = gy // NZ, gy % NZ
    right, left = (gx + 1) % count_x, (gx + count_x - 1) % count_x
    after, before = (gy + 1) % count_y, (gy + count_y - 1) % count_y
    first, last = gx == 0, gx == count_x - 1

    loads = [
        pltpu.make_async_copy(source, target, load_sem.at[i])
        for i, (source, target) in enumerate(
            (
                (heights_hbm, heights),
                (prec_hbm, prec),
                (u_hbm, u),
                (v_hbm, v),
                (w_hbm, w),
                (vert_hbm, vert_f32),
                (inv_hbm.at[gy], inv),
                (span_hbm, span_f32),
            )
        )
    ]
    for load in loads:
        load.start()

    barrier = pltpu.get_barrier_semaphore()

    def greet(other, _):
        @pl.when(other != gy)
        def _():
            pl.semaphore_signal(barrier, inc=1, device_id={"gy": other}, device_id_type=MESH)

        return 0

    lax.fori_loop(0, count_y, greet, 0)
    pl.semaphore_signal(barrier, inc=1, device_id={"gx": right}, device_id_type=MESH)
    pl.semaphore_signal(barrier, inc=1, device_id={"gx": left}, device_id_type=MESH)

    @pl.when(first)
    def _():
        for other in (before, after):
            pl.semaphore_signal(barrier, inc=1, device_id={"gx": left, "gy": other}, device_id_type=MESH)

    rows, levels = u.shape[1], u.shape[2]
    planes = u.shape[0]
    half = planes // 2
    for load in loads[:4]:
        load.wait()
    tall = heights[...].astype(F32).T
    level = lax.broadcasted_iota(jnp.int32, (rows, levels), 1).astype(F32)

    def opened(x):
        return level >= tall[:, x : x + 1]

    u_out[...] = jnp.where(last, prec[0, 2], jnp.where(opened(planes - 1), u[planes - 1], 0.0))
    for x in range(planes):
        south_out[x : x + 1] = jnp.where(opened(x)[rows - 1 :], v[x, rows - 1 : rows], 0.0)
    for c in range(3):
        for x in range(4):
            south_out[planes + 4 * c + x : planes + 4 * c + x + 1] = prec[c, x, rows - 1 : rows]
            north_out[4 * c + x : 4 * c + x + 1] = prec[c, x, 0:1]

    loads[5].wait()
    vert_rows = vert_f32.shape[0]
    vert[:vert_rows], vert[vert_rows:] = split(vert_f32[...])

    pl.semaphore_wait(barrier, count_y + 1 + jnp.where(last, 2, 0))

    def remote(source, target, i, device):
        return pltpu.make_async_remote_copy(
            source, target, halo_send.at[i], halo_recv.at[i], device_id=device, device_id_type=MESH
        )

    halos = [
        remote(south_out, south_in, 0, {"gy": after}),
        remote(u_out, u_in, 1, {"gx": right}),
        remote(prec.at[:, 3], west_in, 2, {"gx": right}),
        remote(north_out, north_in, 3, {"gy": before}),
        remote(prec.at[:, 0], east_in, 4, {"gx": left}),
    ]
    corners = [
        remote(prec.at[0, 3, pl.ds(rows - 8, 8)], corner_in.at[0], 5, {"gx": right, "gy": after}),
        remote(prec.at[0, 3, pl.ds(0, 8)], corner_in.at[1], 6, {"gx": right, "gy": before}),
    ]

    @pl.when(last)
    def _():
        for copy in corners:
            copy.start()

    for copy in halos:
        copy.start()

    loads[4].wait()
    places = {}
    for c, members in enumerate(CHUNKS):
        for i, x in enumerate(members):
            places[x] = (8 * c + i) * rows
    u_prev = None
    zero_row = jnp.zeros((1, levels), F32)
    for x in range(planes):
        is_open = opened(x)
        u_open = jnp.where(is_open, u[x], 0.0)
        v_open = jnp.where(is_open, v[x], 0.0)
        w_open = jnp.where(is_open, w[x], 0.0)
        u_step = u_open if x == 0 else u_open - u_prev
        value = u_step + (v_open - row_shift(v_open, zero_row, False)) + (w_open - lane_shift(w_open, False))
        rhs[pl.ds(places[x % half], rows), pl.ds(x // half * levels, levels)] = -value
        u_prev = u_open

    halos[0].wait_recv()
    halos[1].wait_recv()

    @pl.when(first)
    def _():
        halos[2].wait_recv()
        for copy in corners:
            copy.wait_recv()
        q, west = west_in[0], u_in[...]
        south = row_shift(q, corner_in[0, 7:8], False)
        north = row_shift(q, corner_in[1, 0:1], True)
        u_before[...] = stencil(q, q, west_in[1], west_in[2], prec[0, 0], west, north, south)

    @pl.when(jnp.logical_not(first))
    def _():
        u_before[...] = u_in[...]


    def transform(c):
        row = lax.broadcasted_iota(jnp.int32, (rows, 2 * levels), 0)
        for i, x in enumerate(CHUNKS[c]):
            here = pl.ds((8 * c + i) * rows, rows)
            value = rhs[here]
            edge = jnp.concatenate([south_in[x : x + 1], south_in[half + x : half + x + 1]], 1)
            value = value + jnp.where(row == 0, edge, 0.0)
            if x == 0:
                value = value + jnp.concatenate([u_before[...], jnp.zeros((rows, levels), F32)], 1)
            rhs_hi[here], rhs_lo[here] = split(value)
        cells = pl.ds(8 * c * rows, 8 * rows)
        dims = (((1,), (1,)), ((), ()))
        main = lax.dot_general(vert[...], rhs_hi[cells], dims, preferred_element_type=F32)
        rest = lax.dot_general(vert[:vert_rows], rhs_lo[cells], dims, preferred_element_type=F32)
        outgoing[c] = main[:vert_rows] + main[vert_rows:] + rest

    def block(c, other):
        return pltpu.make_async_remote_copy(
            outgoing.at[c, pl.ds(pl.multiple_of(8 * other, 8), 8)],
            incoming.at[c, my_z, my_y],
            send_sem.at[c, other],
            recv_sem.at[c, gy],
            device_id={"gy": other},
            device_id_type=MESH,
        )

    def send(c, z):
        def one(i, _):
            other = (my_y + i) % NY * NZ + z

            @pl.when(other != gy)
            def _():
                block(c, other).start()

            return 0

        lax.fori_loop(0, NY, one, 0)

    for c in range(2):
        transform(c)
        send(c, 0)
        incoming[c, my_z, my_y] = outgoing[c, pl.ds(pl.multiple_of(8 * gy, 8), 8)]
    for z in range(1, NZ):
        for c in range(2):
            send(c, z)

    @pl.when(jnp.logical_not(first))
    def _():
        halos[2].wait_recv()

    halos[3].wait_recv()
    halos[4].wait_recv()
    for x in range(4):
        a, b, c = prec[0, x], prec[1, x], prec[2, x]
        for k in range(3):
            q = prec[k, x]
            west = west_in[k] if x == 0 else prec[k, x - 1]
            east = east_in[k] if x == 3 else prec[k, x + 1]
            place = 4 * k + x
            south = row_shift(q, south_in[planes + place : planes + place + 1], False)
            north = row_shift(q, north_in[place : place + 1], True)
            next_v[k, x] = stencil(q, a, b, c, east, west, north, south)
    next_store = pltpu.make_async_copy(next_v, next_hbm, store_sem.at[0])
    next_store.start()

    for load in loads[6:]:
        load.wait()

    def split_span(i, _):
        for z in range(NZ):
            here = pl.ds(pl.multiple_of(i * 32, 32), 32)
            span_hi[z, here], span_lo[z, here] = split(span_f32[z, here])
        return 0

    lax.fori_loop(0, span_f32.shape[1] // 32, split_span, 0)

    lane = lax.broadcasted_iota(jnp.int32, (8, 128), 1)
    low_half, even_block = lane < 64, lane // 32 % 2 == 0

    def regrouped(c, z):
        columns = []
        for y0 in (0, 4):
            cells = []
            for x0 in (0, 128):
                s = [incoming[c, z, y0 + i, :, x0 : x0 + 128] for i in range(4)]
                for i in (0, 1):
                    s[i], s[i + 2] = (
                        jnp.where(low_half, s[i], pltpu.roll(s[i + 2], 64, 1)),
                        jnp.where(low_half, pltpu.roll(s[i], 64, 1), s[i + 2]),
                    )
                for i in (0, 2):
                    s[i], s[i + 1] = (
                        jnp.where(even_block, s[i], pltpu.roll(s[i + 1], 32, 1)),
                        jnp.where(even_block, pltpu.roll(s[i], 96, 1), s[i + 1]),
                    )
                cells += s
            columns.append(jnp.concatenate(cells, 0))
        return jnp.concatenate(columns, 1)

    def receive(c, step):
        z = (my_z + step) % NZ

        def one(i, _):
            other = i * NZ + z

            @pl.when(other != gy)
            def _():
                block_in = pltpu.make_async_remote_copy(
                    outgoing.at[c, pl.ds(pl.multiple_of(8 * other, 8), 8)],
                    incoming.at[c, z, i],
                    send_sem.at[c, other],
                    recv_sem.at[c, other],
                    device_id={"gy": other},
                    device_id_type=MESH,
                )
                block_in.wait_recv()

            return 0

        lax.fori_loop(0, NY, one, 0)
        high, low = split(regrouped(c, z))
        count = high.shape[0]
        both = jnp.concatenate([high, low], 0)
        main = jnp.dot(both, span_hi[z], preferred_element_type=F32)
        rest = jnp.dot(high, span_lo[z], preferred_element_type=F32)
        return main[:count] + main[count:] + rest

    width = span_hi.shape[2]

    def place(c, total, add):
        total = total.reshape(8, 8, width)
        pieces = ((3, 0, 4), (15, 4, 8)) if c == 0 else ((7, 0, 8),)
        for at, begin, end in pieces:
            here = pl.ds(at, end - begin)
            bands[here] = bands[here] + total[begin:end] if add else total[begin:end]

    def edge(i, source, target, device):
        return pltpu.make_async_remote_copy(
            source, target, edge_send.at[i], edge_recv.at[i], device_id=device, device_id_type=MESH
        )

    to_right = edge(0, bands.at[pl.ds(16, 3)], left_in, {"gx": right})
    to_left = edge(1, bands.at[pl.ds(3, 3)], right_in, {"gx": left})

    for c in range(2):
        for step in (0, 1, 3, 2):
            place(c, receive(c, step), step != 0)
        if c == 0:

            @pl.when(jnp.logical_not(last))
            def _():
                to_right.start()

            @pl.when(jnp.logical_not(first))
            def _():
                to_left.start()

    @pl.when(jnp.logical_not(first))
    def _():
        to_right.wait_recv()

    @pl.when(first)
    def _():
        left_in[...] = jnp.zeros_like(left_in)

    @pl.when(jnp.logical_not(last))
    def _():
        to_left.wait_recv()

    @pl.when(last)
    def _():
        right_in[...] = jnp.zeros_like(right_in)

    even = lax.broadcasted_iota(jnp.int32, (8, 128), 0) % 2 == 0
    inside_left = jnp.where(jnp.logical_and(even, first), 0.0, 1.0)
    inside_right = jnp.where(jnp.logical_and(jnp.logical_not(even), last), 0.0, 1.0)
    for lane0 in range(0, width, 128):
        lanes = pl.ds(lane0, 128)
        scale = inv[:, lanes]
        left_scale, right_scale = scale * inside_left, scale * inside_right
        b = [None] * 22
        for i in range(3):
            b[i] = jnp.where(even, pltpu.roll(left_in[i, :, lanes], 7, 0), pltpu.roll(bands[16 + i, :, lanes], 1, 0))
            b[19 + i] = jnp.where(even, pltpu.roll(bands[3 + i, :, lanes], 7, 0), pltpu.roll(right_in[i, :, lanes], 1, 0))
        for i in range(3, 19):
            b[i] = bands[i, :, lanes]
        scales = [left_scale] * 3 + [scale] * 16 + [right_scale] * 3
        p = [b[i] * scales[i] for i in range(22)]
        for turn in range(1, ITERS):
            inner = range(turn, 22 - turn)
            new = [None] * 22
            for i in inner:
                new[i] = (b[i] + p[i - 1] + p[i + 1]) * scales[i]
            p = new
        for i in range(16):
            solved[i, :, lanes] = p[3 + i]

    mirror = (128 - lane) % 128
    origin = lane == 0
    pieces = width // 256
    for i in range(16):
        here = pl.ds(i, 8, stride=half)
        parts = [solved[i, :, 128 * k : 128 * k + 128] for k in range(2 * pieces)]
        turned = [jnp.take_along_axis(part, mirror, axis=1) for part in parts]
        for k in range(pieces):
            press_v[0, k, here] = parts[k]
            press_v[0, pieces + k, here] = jnp.where(origin, turned[pieces - k], turned[pieces - k - 1])
            part = parts[pieces + k]
            press_v[1, k, here] = jnp.where(origin, 0.0, part) if k == 0 else part
            beyond = turned[2 * pieces - k] if k else jnp.zeros_like(part)
            press_v[1, pieces + k, here] = -jnp.where(origin, beyond, turned[2 * pieces - k - 1])
    stores = [
        pltpu.make_async_copy(
            press_v.at[part, k],
            press_hbm.at[part, :, pl.ds(128 * k, 128)],
            store_sem.at[1 + 2 * pieces * part + k],
        )
        for part in range(2)
        for k in range(2 * pieces)
    ]
    for store in stores:
        store.start()

    for copy in halos:
        copy.wait_send()

    @pl.when(last)
    def _():
        for copy in corners:
            copy.wait_send()

    @pl.when(jnp.logical_not(last))
    def _():
        to_right.wait_send()

    @pl.when(jnp.logical_not(first))
    def _():
        to_left.wait_send()

    def sent(other, _):
        @pl.when(other != gy)
        def _():
            for c in range(2):
                block(c, other).wait_send()

        return 0

    lax.fori_loop(0, count_y, sent, 0)
    next_store.wait()
    for store in stores:
        store.wait()


def on_device(precursor, u_star, v_star, w_star, heights):
    planes, rows, levels = u_star.shape
    groups = lax.axis_size("gy")
    width = rows * groups
    vert = vertical_tables(levels, groups)
    span = span_tables(width)
    inv = inverse_diagonal(levels, width, groups)
    half = planes // 2
    per = 2 * levels // groups
    any_space = pl.BlockSpec(memory_space=pl.ANY)
    vmem = pltpu.VMEM
    dma = pltpu.SemaphoreType.DMA
    precursor_next, pressure = pl.pallas_call(
        kernel,
        out_shape=(
            jax.ShapeDtypeStruct(precursor.shape, F32),
            jax.ShapeDtypeStruct((2, levels // groups * planes, width), F32),
        ),
        in_specs=[any_space] * 8,
        out_specs=(any_space, any_space),
        scratch_shapes=[
            vmem(precursor.shape, F32),
            vmem(u_star.shape, F32),
            vmem(u_star.shape, F32),
            vmem(u_star.shape, F32),
            vmem(heights.shape, jnp.int32),
            vmem(vert.shape, F32),
            vmem(span.shape, F32),
            vmem((per, width), F32),
            vmem((2 * vert.shape[0], vert.shape[1]), BF16),
            vmem(span.shape, BF16),
            vmem(span.shape, BF16),
            vmem((rows, levels), F32),
            vmem((planes + 16, levels), F32),
            vmem((16, levels), F32),
            vmem((rows, levels), F32),
            vmem((planes + 16, levels), F32),
            vmem((16, levels), F32),
            vmem((3, rows, levels), F32),
            vmem((3, rows, levels), F32),
            vmem((2, 8, levels), F32),
            vmem((rows, levels), F32),
            vmem((half * rows, 2 * levels), F32),
            vmem((half * rows, 2 * levels), BF16),
            vmem((half * rows, 2 * levels), BF16),
            vmem((2, 2 * levels, half * rows // 2), F32),
            vmem((2, NZ, NY, per, half * rows // 2), F32),
            vmem((half + 6, per, width), F32),
            vmem((3, per, width), F32),
            vmem((3, per, width), F32),
            vmem((half, per, width), F32),
            vmem(precursor.shape, F32),
            vmem((2, width // 128, levels // groups * planes, 128), F32),
            dma((8,)),
            dma((7,)),
            dma((7,)),
            dma((2, groups)),
            dma((2, groups)),
            dma((2,)),
            dma((2,)),
            dma((1 + 2 * width // 128,)),
        ],
        compiler_params=pltpu.CompilerParams(
            collective_id=0, has_side_effects=True, vmem_limit_bytes=56 * 2**20
        ),
        name="section",
    )(precursor, u_star, v_star, w_star, heights, vert, span, inv)
    return precursor_next, pressure.reshape(2, levels // groups, planes, width)


def solution(mesh):
    placed = (
        P(None, "gx", "gy", None),
        P("gx", "gy", None),
        P("gx", "gy", None),
        P("gx", "gy", None),
        P("gx", "gy"),
    )
    return jax.shard_map(
        on_device,
        mesh=mesh,
        in_specs=placed,
        out_specs=(P(None, "gx", "gy", None), P(None, "gy", "gx", None)),
        check_vma=False,
    )
```

time: 159 us -> 54.9 us (0.35)
  the two profiles are of different devices: /device:TPU:79 before, /device:TPU:199 now
where the time goes in v1:
time: 54.9 us; the launch traced here: 54.7 us
  Pallas kernels  50.1 us (91%)
  local copies, waits for them, and re-layouts  3.92 us (7%)
  between operations  0.64 us (1%)
    pallas_call x1, Pallas kernels, on_device(): pl.pallas_call(kernel, out_shape=(jax.ShapeDtypeStruct(precursor.shape, F...  50.1 us
    unnamed x2, local copies, waits for them, and re-layouts  3.92 us

profile of v1, /device:TPU:199, one launch (start us, length us, event | category | flops | bytes accessed | tf_op | source)
XLA Modules:
  0.0 54.7 jit_solution(8256560727652108911)
XLA Ops:
  0.6 50.1 %section.1 = (f32[3,4,32,128]{3,2,1,0:T(8,128)}, f32[2,128,1024]{2,1,0:T(8,128)}) custom-call(f32[3,4,32,128]{3,2,1,0:T(8,128)} %prec_hbm.1, f32[32,32,128]{2,1,0:T(8,128)} %u_hbm.1, f32[32,32,128]{2,1,0:T(8,128)} %v_hbm.1, f32[32,32,128]{2,1,0:T(8,128)} %w_hbm.1, s32[32,32]{1,0:T(8,128)} %heights_hbm.1, f32[256,256]{1,0:T(8,128)} %constant.6.clone.vert_hbm, ...), custom_call_target="tpu_custom_call" | custom-call | tf_op jit(solution)/shard_map/section/pallas_call | solution.py:481
  50.7 1.6 %copy.12 = f32[3,4,32,128]{3,2,1,0:T(8,128)} copy(f32[3,4,32,128]{3,2,1,0:T(8,128)} %get-tuple-element.8) | data formatting | bytes 393216
  52.4 2.3 %copy.13 = f32[2,4,32,1024]{3,2,1,0:T(8,128)} copy(f32[2,4,32,1024]{3,2,1,0:T(8,128)} %bitcast.1) | data formatting | bytes 2097152

commit v2 on v1

v2 whole, which is shorter than its diff:
```python
import functools
import math

import jax
import jax.numpy as jnp
import numpy as np
from jax import lax
from jax.experimental import pallas as pl
from jax.experimental.pallas import tpu as pltpu
from jax.sharding import PartitionSpec as P

ITERS = 4
NY = 8
NZ = 4
MESH = pl.DeviceIdType.MESH
F32 = jnp.float32
BF16 = jnp.bfloat16
CHUNKS = ((0, 1, 2, 3, 12, 13, 14, 15), (4, 5, 6, 7, 8, 9, 10, 11))


def split(value):
    high = value.astype(BF16)
    return high, (value - high.astype(F32)).astype(BF16)


def vertical_tables(levels, groups):
    modes = np.arange(levels)[:, None]
    cells = np.arange(levels)[None, :]
    weight = np.where(modes == 0, 1.0, 2.0) / levels
    table = np.sqrt(weight) * np.cos(modes * (2 * cells + 1) % (4 * levels) * (math.pi / (2 * levels)))
    both = np.zeros((levels, 2, 2, levels))
    both[:, 0, 0] = table
    both[:, 1, 1] = table
    return both.reshape(2 * levels, 2 * levels).astype(np.float32)


def side_table(levels, groups):
    modes = np.arange(levels)[:, None]
    cells = np.arange(levels)[None, :]
    weight = np.where(modes == 0, 1.0, 2.0) / levels
    table = np.sqrt(weight) * np.cos(modes * (2 * cells + 1) % (4 * levels) * (math.pi / (2 * levels)))
    return table.reshape(groups, -1).astype(np.float32)


def span_tables(width):
    half = width // 2
    y = np.arange(width)[:, None]
    cos = np.cos(y * np.arange(half + 1)[None] % width * (2 * math.pi / width))
    sin = np.sin(y * np.arange(1, half)[None] % width * (2 * math.pi / width))
    table = np.concatenate([cos, -sin], 1) / math.sqrt(width)
    cells = width // (NY * NZ)
    after = np.roll(table[::cells], -1, 0).reshape(NY, NZ, width).transpose(1, 0, 2).reshape(NY * NZ, width)
    table = table.reshape(NY, NZ, cells, width).transpose(1, 0, 2, 3).reshape(NZ, NY * cells, width)
    return table.astype(np.float32), after.astype(np.float32)


def inverse_diagonal(levels, width, groups):
    modes = np.arange(levels).reshape(groups, levels // groups, 1, 1)
    half = width // 2
    waves = np.concatenate([np.arange(half + 1), np.arange(1, half)])
    diagonal = 6.0 - 2.0 * np.cos(modes * (math.pi / levels)) - 2.0 * np.cos(waves * (2 * math.pi / width))
    both = np.broadcast_to(1.0 / diagonal, (groups, levels // groups, 2, width))
    return both.reshape(groups, 2 * levels // groups, width).astype(np.float32)


def lane_shift(value, up):
    levels = value.shape[1]
    lane = lax.broadcasted_iota(jnp.int32, value.shape, 1)
    if up:
        return jnp.where(lane == levels - 1, 0.0, pltpu.roll(value, levels - 1, 1))
    return jnp.where(lane == 0, 0.0, pltpu.roll(value, 1, 1))


def row_shift(value, edge, up):
    count = value.shape[0]
    row = lax.broadcasted_iota(jnp.int32, value.shape, 0)
    if up:
        return jnp.where(row == count - 1, edge, pltpu.roll(value, count - 1, 0))
    return jnp.where(row == 0, edge, pltpu.roll(value, 1, 0))


def stencil(q, a, b, c, east, west, north, south):
    above = lane_shift(q, True)
    below = lane_shift(q, False)
    advect = a * (east - west) * 0.5 + b * (north - south) * 0.5 + c * (above - below) * 0.5
    spread = east + west + north + south + above + below - 6.0 * q
    return q + 0.1 * (0.2 * spread - advect)


def three_pass(main, rest, count):
    return main[:count] + main[count:] + rest


def kernel(
    prec_hbm, u_hbm, v_hbm, w_hbm, heights_hbm, vert_hbm, side_hbm, after_hbm, span_hbm,
    next_hbm, bands_hbm, left_hbm, right_hbm, beyond_hbm,
    prec, u, v, w, heights, vert_f32, side_f32, after_f32, span_f32, vert, span_hi, span_lo,
    south_out, north_out, south_in, north_in, west_in, east_in,
    spread, side_out, side_in, side_v, side_u, side_rows,
    rhs, rhs_hi, rhs_lo, outgoing, incoming, bands, beyond, left_out, right_out, left_in, right_in, next_v,
    load_sem, halo_send, halo_recv, side_send, side_recv, send_sem, recv_sem, edge_send, edge_recv, store_sem, late_in, all_in,
):
    gx, gy = lax.axis_index("gx"), lax.axis_index("gy")
    count_x, count_y = lax.axis_size("gx"), lax.axis_size("gy")
    my_y, my_z = gy // NZ, gy % NZ
    right, left = (gx + 1) % count_x, (gx + count_x - 1) % count_x
    after, before = (gy + 1) % count_y, (gy + count_y - 1) % count_y
    first, last = gx == 0, gx == count_x - 1
    early = my_z < 2

    loads = [
        pltpu.make_async_copy(source, target, load_sem.at[i])
        for i, (source, target) in enumerate(
            (
                (prec_hbm, prec),
                (heights_hbm, heights),
                (u_hbm, u),
                (v_hbm, v),
                (w_hbm, w),
                (vert_hbm, vert_f32),
                (side_hbm, side_f32),
                (after_hbm, after_f32),
                (span_hbm, span_f32),
            )
        )
    ]
    for load in loads:
        load.start()

    barrier = pltpu.get_barrier_semaphore()

    def greet_line(sem, zs):
        for z in zs:

            def greet(y, _):
                other = y * NZ + z

                @pl.when(other != gy)
                def _():
                    pl.semaphore_signal(sem, inc=1, device_id={"gy": other}, device_id_type=MESH)

                return 0

            lax.fori_loop(0, NY, greet, 0)

    pl.semaphore_signal(barrier, inc=1, device_id={"gx": right}, device_id_type=MESH)
    pl.semaphore_signal(barrier, inc=1, device_id={"gx": left}, device_id_type=MESH)

    @pl.when(early)
    def _():
        greet_line(barrier, (2, 3, 0, 1))

    @pl.when(my_z == 2)
    def _():
        greet_line(barrier, (3,))
        pl.semaphore_wait(barrier, 2 * NY + 2)
        greet_line(late_in.at[0], (0, 1))

    @pl.when(my_z == 3)
    def _():
        pl.semaphore_wait(barrier, 3 * NY + 2)
        greet_line(late_in.at[1], (0, 1, 2))

    rows, levels = u.shape[1], u.shape[2]
    planes = u.shape[0]
    half = planes // 2
    loads[0].wait()
    for c in range(3):
        for x in range(4):
            south_out[4 * c + x : 4 * c + x + 1] = prec[c, x, rows - 1 : rows]
            north_out[4 * c + x : 4 * c + x + 1] = prec[c, x, 0:1]

    def remote(source, target, i, device):
        return pltpu.make_async_remote_copy(
            source, target, halo_send.at[i], halo_recv.at[i], device_id=device, device_id_type=MESH
        )

    halos = [
        remote(south_out, south_in, 0, {"gy": after}),
        remote(north_out, north_in, 1, {"gy": before}),
        remote(prec.at[:, 3], west_in, 2, {"gx": right}),
        remote(prec.at[:, 0], east_in, 3, {"gx": left}),
    ]

    def send_halos(south, north):
        halos[2].start()
        halos[3].start()

        @pl.when(south)
        def _():
            halos[0].start()

        @pl.when(north)
        def _():
            halos[1].start()

    @pl.when(jnp.logical_not(early))
    def _():
        send_halos(my_z == 3, my_z >= 2)

    spread[...] = jnp.zeros_like(spread)
    for load in loads[1:5]:
        load.wait()
    tall = heights[...].astype(F32).T
    level = lax.broadcasted_iota(jnp.int32, (rows, levels), 1).astype(F32)
    places = {}
    for c, members in enumerate(CHUNKS):
        for i, x in enumerate(members):
            places[x] = (8 * c + i) * rows
    u_prev = None
    zero_row = jnp.zeros((1, levels), F32)
    for x in range(planes):
        is_open = level >= tall[:, x : x + 1]
        u_open = jnp.where(is_open, u[x], 0.0)
        v_open = jnp.where(is_open, v[x], 0.0)
        w_open = jnp.where(is_open, w[x], 0.0)
        u_step = u_open if x == 0 else u_open - u_prev
        value = u_step + (v_open - row_shift(v_open, zero_row, False)) + (w_open - lane_shift(w_open, False))
        rhs[pl.ds(places[x % half], rows), pl.ds(x // half * levels, levels)] = -value
        u_prev = u_open
        for m in range(4):
            at = 8 * (x % half) + 2 * m + x // half
            spread[m, at : at + 1] = v_open[rows - 1 :]

    def side(plane):
        for m in range(4):
            spread[m, 4 * rows + m * rows : 4 * rows + (m + 1) * rows] = plane
        table = side_f32[...]
        count = table.shape[0]
        table_hi, table_lo = split(table)
        value_hi, value_lo = split(jnp.concatenate([spread[m] for m in range(4)], 1))
        dims = (((1,), (1,)), ((), ()))
        main = lax.dot_general(jnp.concatenate([table_hi, table_lo], 0), value_hi, dims, preferred_element_type=F32)
        rest = lax.dot_general(table_hi, value_lo, dims, preferred_element_type=F32)
        value = three_pass(main, rest, count)
        for p in range(count):
            side_out[p, 0:1] = value[p : p + 1, :128]
            side_out[p, 1:2] = value[p : p + 1, 128:]
        side_in[my_z, my_y] = side_out[gy]

    loads[5].wait()
    loads[6].wait()
    vert_rows = vert_f32.shape[0]
    vert[:vert_rows], vert[vert_rows:] = split(vert_f32[...])

    def transform(c):
        for i in range(8):
            here = pl.ds((8 * c + i) * rows, rows)
            rhs_hi[here], rhs_lo[here] = split(rhs[here])
        cells = pl.ds(8 * c * rows, 8 * rows)
        dims = (((1,), (1,)), ((), ()))
        main = lax.dot_general(vert[...], rhs_hi[cells], dims, preferred_element_type=F32)
        rest = lax.dot_general(vert[:vert_rows], rhs_lo[cells], dims, preferred_element_type=F32)
        outgoing[c] = three_pass(main, rest, vert_rows)
        incoming[c, my_z, my_y] = outgoing[c, pl.ds(pl.multiple_of(8 * gy, 8), 8)]

    def block(c, other, z, y):
        return pltpu.make_async_remote_copy(
            outgoing.at[c, pl.ds(pl.multiple_of(8 * other, 8), 8)],
            incoming.at[c, z, y],
            send_sem.at[c, other],
            recv_sem.at[c, z * NY + y],
            device_id={"gy": other},
            device_id_type=MESH,
        )

    def side_block(other, z, y):
        return pltpu.make_async_remote_copy(
            side_out.at[other],
            side_in.at[z, y],
            side_send.at[other],
            side_recv.at[z * NY + y],
            device_id={"gy": other},
            device_id_type=MESH,
        )

    def send(make, z):
        def one(i, _):
            other = (my_y + i) % NY * NZ + z

            @pl.when(other != gy)
            def _():
                make(other, my_z, my_y).start()

            return 0

        lax.fori_loop(0, NY, one, 0)

    def send_side(z):
        @pl.when(jnp.logical_not(last))
        def _():
            send(side_block, z)

    side(u_prev)
    transform(0)

    def split_tables():
        loads[7].wait()
        loads[8].wait()

        def split_span(i, _):
            for z in range(NZ):
                here = pl.ds(pl.multiple_of(i * 32, 32), 32)
                span_hi[z, here], span_lo[z, here] = split(span_f32[z, here])
            return 0

        lax.fori_loop(0, span_f32.shape[1] // 32, split_span, 0)

    @pl.when(early)
    def _():
        split_tables()
        pl.semaphore_wait(barrier, 2 * NY + 1)
        send_halos(my_z == 0, my_z == 1)

    def send_middle(z):
        @pl.when(jnp.logical_not(last))
        def _():
            send(functools.partial(block, 1), z)

    def send_all(z):
        send_side(z)
        send(functools.partial(block, 0), z)
        send_middle(z)

    for z in (0, 1):
        send_side(z)
        send(functools.partial(block, 0), z)
    transform(1)
    for z in (0, 1):
        send_middle(z)

    @pl.when(early)
    def _():
        pl.semaphore_wait(late_in.at[0], NY)

    @pl.when(my_z == 0)
    def _():
        pl.semaphore_signal(all_in, inc=1, device_id={"gy": my_y * NZ + 2}, device_id_type=MESH)

    @pl.when(my_z == 1)
    def _():
        halos[0].start()

    @pl.when(my_z != 2)
    def _():
        send_all(2)

    @pl.when(my_z != 3)
    def _():
        pl.semaphore_wait(late_in.at[1], NY)

    @pl.when(my_z == 0)
    def _():
        pl.semaphore_signal(all_in, inc=1, device_id={"gy": my_y * NZ + 3}, device_id_type=MESH)
        halos[1].start()

    @pl.when(my_z == 2)
    def _():
        halos[0].start()

    @pl.when(my_z != 3)
    def _():
        send_all(3)

    @pl.when(jnp.logical_not(early))
    def _():
        split_tables()

    for copy in halos:
        copy.wait_recv()
    for x in (3, 2, 1, 0):
        a, b, c = prec[0, x], prec[1, x], prec[2, x]
        for k in range(3):
            q = prec[k, x]
            west = west_in[k] if x == 0 else prec[k, x - 1]
            east = east_in[k] if x == 3 else prec[k, x + 1]
            place = 4 * k + x
            south = row_shift(q, south_in[place : place + 1], False)
            north = row_shift(q, north_in[place : place + 1], True)
            next_v[k, x] = stencil(q, a, b, c, east, west, north, south)
    next_store = pltpu.make_async_copy(next_v, next_hbm, store_sem.at[0])
    next_store.start()

    @pl.when(last)
    def _():
        side(next_v[0, 3])
        for z in range(NZ):

            @pl.when(jnp.logical_or(early, my_z != z))
            def _():
                send(side_block, z)

        for z in range(NZ):

            @pl.when(jnp.logical_or(early, my_z != z))
            def _():
                send(functools.partial(block, 1), z)

    for z in (2, 3):

        @pl.when(my_z == z)
        def _():
            pl.semaphore_wait(all_in, 1)
            send(side_block, z)
            for c in range(2):
                send(functools.partial(block, c), z)

    side_u[...] = jnp.zeros_like(side_u)
    side_rows[...] = jnp.zeros_like(side_rows)

    lane = lax.broadcasted_iota(jnp.int32, (8, 128), 1)
    low_half, even_block = lane < 64, lane // 32 % 2 == 0

    def exchanged(s):
        s = list(s)
        for i in (0, 1):
            s[i], s[i + 2] = (
                jnp.where(low_half, s[i], pltpu.roll(s[i + 2], 64, 1)),
                jnp.where(low_half, pltpu.roll(s[i], 64, 1), s[i + 2]),
            )
        for i in (0, 2):
            s[i], s[i + 1] = (
                jnp.where(even_block, s[i], pltpu.roll(s[i + 1], 32, 1)),
                jnp.where(even_block, pltpu.roll(s[i], 96, 1), s[i + 1]),
            )
        return s

    def regrouped(c, z):
        columns = []
        for y0 in (0, 4):
            cells = []
            for x0 in (0, 128):
                cells += exchanged([incoming[c, z, y0 + i, :, x0 : x0 + 128] for i in range(4)])
            columns.append(jnp.concatenate(cells, 0))
        return jnp.concatenate(columns, 1)

    def sides(z):
        for y in range(NY):
            both = side_in[z, y]
            side_v[pl.ds(z * NY + y, 1)] = both[0:1]
            at = 8 * (y % 4) + y // 4
            side_u[at : at + 1] = both[1:2]
        found = exchanged([side_u[8 * i : 8 * i + 8] for i in range(4)])
        for m in range(4):
            for y0 in range(2):
                side_rows[y0, 2 * m + 1 : 2 * m + 2] = found[m][y0 : y0 + 1]
        return jnp.concatenate([side_rows[0], side_rows[1]], 1)

    def arrived(make, z):
        def one(i, _):
            other = i * NZ + z

            @pl.when(other != gy)
            def _():
                make(other, z, i).wait_recv()

            return 0

        lax.fori_loop(0, NY, one, 0)

    def receive(c, step):
        z = step if step < 2 else jnp.where(my_z == 2, 5 - step, step)
        if c == 0:
            arrived(side_block, z)
        arrived(functools.partial(block, c), z)
        value = regrouped(c, z)
        if c == 0:
            value = jnp.concatenate([value, sides(z)], 0)
        high, low = split(value)
        main = jnp.dot(jnp.concatenate([high, low], 0), span_hi[z], preferred_element_type=F32)
        rest = jnp.dot(high, span_lo[z], preferred_element_type=F32)
        return three_pass(main, rest, value.shape[0])

    width = span_hi.shape[2]
    even = lax.broadcasted_iota(jnp.int32, (8, width), 0) % 2 == 0

    def edge(i, source, target, device):
        return pltpu.make_async_remote_copy(
            source, target, edge_send.at[i], edge_recv.at[i], device_id=device, device_id_type=MESH
        )

    to_right = edge(0, left_out, left_in, {"gx": right})
    to_left = edge(1, right_out, right_in, {"gx": left})

    for i, step in enumerate(range(NZ)):
        total = receive(0, step)
        for k, x in enumerate(CHUNKS[0]):
            part = total[8 * k : 8 * k + 8]
            bands[x] = part if i == 0 else bands[x] + part
        part = total[64:72]
        beyond[...] = part if i == 0 else beyond[...] + part
    high, low = split(side_v[...].T)
    after_hi, after_lo = split(after_f32[...])
    count = high.shape[0]
    total = three_pass(
        jnp.dot(jnp.concatenate([high, low], 0), after_hi, preferred_element_type=F32),
        jnp.dot(high, after_lo, preferred_element_type=F32),
        count,
    )
    for x in range(half):
        part = total[8 * x : 8 * x + 8]
        bands[x] = bands[x] + part if x in CHUNKS[0] else part
    left_out[0] = jnp.where(even, pltpu.roll(bands[half - 3], 7, 0), bands[half - 2])
    left_out[1] = jnp.where(even, pltpu.roll(bands[half - 1], 7, 0), beyond[...])
    right_out[0] = jnp.where(even, bands[0], pltpu.roll(bands[1], 1, 0))
    right_out[1] = bands[2]
    to_right.start()

    @pl.when(jnp.logical_not(first))
    def _():
        to_left.start()

    for step in range(NZ):
        total = receive(1, step)
        for k, x in enumerate(CHUNKS[1]):
            bands[x] = bands[x] + total[8 * k : 8 * k + 8]

    stores = [
        pltpu.make_async_copy(bands, bands_hbm, store_sem.at[1]),
        pltpu.make_async_copy(beyond, beyond_hbm, store_sem.at[2]),
        pltpu.make_async_copy(left_in, left_hbm, store_sem.at[3]),
        pltpu.make_async_copy(right_in, right_hbm, store_sem.at[4]),
    ]
    stores[0].start()
    stores[1].start()
    to_right.wait_recv()
    stores[2].start()

    @pl.when(jnp.logical_not(last))
    def _():
        to_left.wait_recv()

    @pl.when(last)
    def _():
        right_in[...] = jnp.zeros_like(right_in)

    stores[3].start()

    for copy in halos:
        copy.wait_send()
    to_right.wait_send()

    @pl.when(jnp.logical_not(first))
    def _():
        to_left.wait_send()

    def sent(other, _):
        @pl.when(other != gy)
        def _():
            side_block(other, my_z, my_y).wait_send()
            for c in range(2):
                block(c, other, my_z, my_y).wait_send()

        return 0

    lax.fori_loop(0, count_y, sent, 0)
    next_store.wait()
    for store in stores:
        store.wait()


def finish(
    next_in, bands_hbm, left_hbm, right_hbm, beyond_hbm, inv_hbm,
    next_hbm, press_hbm,
    bands, left_in, right_in, beyond, inv, next_v, solved, press_v,
    load_sem, store_sem,
):
    gx, gy = lax.axis_index("gx"), lax.axis_index("gy")
    first, last = gx == 0, gx == lax.axis_size("gx") - 1
    width = inv.shape[1]
    half = bands.shape[0]
    loads = [
        pltpu.make_async_copy(source, target, load_sem.at[i])
        for i, (source, target) in enumerate(
            (
                (bands_hbm, bands),
                (left_hbm, left_in),
                (right_hbm, right_in),
                (beyond_hbm, beyond),
                (inv_hbm.at[gy], inv),
                (next_in, next_v),
            )
        )
    ]
    for load in loads:
        load.start()
    for load in loads:
        load.wait()
    next_store = pltpu.make_async_copy(next_v, next_hbm, load_sem.at[6])
    next_store.start()

    lane = lax.broadcasted_iota(jnp.int32, (8, 128), 1)
    even = lax.broadcasted_iota(jnp.int32, (8, 128), 0) % 2 == 0
    inside_left = jnp.where(jnp.logical_and(even, first), 0.0, 1.0)
    inside_right = jnp.where(jnp.logical_and(jnp.logical_not(even), last), 0.0, 1.0)
    mirror = (128 - lane) % 128
    origin = lane == 0
    pieces = width // 256

    def solve(lane0):
        lanes = pl.ds(lane0, 128)
        scale = inv[:, lanes]
        left_scale, right_scale = scale * inside_left, scale * inside_right
        b = [bands[max(i - 3, 0) if i < 19 else 0, :, lanes] for i in range(22)]
        before = [left_in[i, :, lanes] for i in range(2)]
        behind = [right_in[i, :, lanes] for i in range(2)]
        add = beyond[:, lanes]
        before = [before[0], pltpu.roll(before[0], 7, 0), before[1], pltpu.roll(before[1], 7, 0)]
        behind = [pltpu.roll(behind[0], 1, 0) + add, behind[0], pltpu.roll(behind[1], 1, 0)]
        b[3] = jnp.where(even, b[3] + before[3], b[3])
        for i in range(3):
            b[i] = jnp.where(even, before[i], pltpu.roll(b[16 + i], 1, 0))
            b[19 + i] = jnp.where(even, pltpu.roll(bands[i, :, lanes], 7, 0), behind[i])
        scales = [left_scale] * 3 + [scale] * 16 + [right_scale] * 3
        p = [b[i] * scales[i] for i in range(22)]
        for turn in range(1, ITERS):
            new = [None] * 22
            for i in range(turn, 22 - turn):
                new[i] = (b[i] + p[i - 1] + p[i + 1]) * scales[i]
            p = new
        for i in range(half):
            solved[i, :, lanes] = p[3 + i]

    def write(part):
        stores = [
            pltpu.make_async_copy(
                press_v.at[part, k],
                press_hbm.at[part, :, pl.ds(128 * k, 128)],
                store_sem.at[2 * pieces * part + k],
            )
            for k in range(2 * pieces)
        ]
        for store in stores:
            store.start()
        return stores

    for k in range(pieces, 2 * pieces):
        solve(128 * k)
    for i in range(half):
        here = pl.ds(i, 8, stride=half)
        parts = [solved[i, :, 128 * k : 128 * k + 128] for k in range(pieces, 2 * pieces)]
        turned = [jnp.take_along_axis(part, mirror, axis=1) for part in parts]
        for k in range(pieces):
            press_v[1, k, here] = parts[k] if k else jnp.where(origin, 0.0, parts[k])
            beyond_part = turned[pieces - k] if k else jnp.zeros_like(parts[k])
            press_v[1, pieces + k, here] = -jnp.where(origin, beyond_part, turned[pieces - k - 1])
    stores = write(1)
    for k in range(pieces):
        solve(128 * k)
    for i in range(half):
        here = pl.ds(i, 8, stride=half)
        parts = [solved[i, :, 128 * k : 128 * k + 128] for k in range(pieces + 1)]
        turned = [jnp.take_along_axis(part, mirror, axis=1) for part in parts]
        for k in range(pieces):
            press_v[0, k, here] = parts[k]
            press_v[0, pieces + k, here] = jnp.where(origin, turned[pieces - k], turned[pieces - k - 1])
    stores += write(0)
    next_store.wait()
    for store in stores:
        store.wait()


def on_device(precursor, u_star, v_star, w_star, heights):
    planes, rows, levels = u_star.shape
    groups = lax.axis_size("gy")
    width = rows * groups
    vert = vertical_tables(levels, groups)
    side = side_table(levels, groups)
    span, after = span_tables(width)
    inv = inverse_diagonal(levels, width, groups)
    half = planes // 2
    per = 2 * levels // groups
    any_space = pl.BlockSpec(memory_space=pl.ANY)
    vmem = pltpu.VMEM
    dma = pltpu.SemaphoreType.DMA
    between = (
        jax.ShapeDtypeStruct(precursor.shape, F32),
        jax.ShapeDtypeStruct((half, per, width), F32),
        jax.ShapeDtypeStruct((2, per, width), F32),
        jax.ShapeDtypeStruct((2, per, width), F32),
        jax.ShapeDtypeStruct((per, width), F32),
    )
    held = pl.pallas_call(
        kernel,
        out_shape=between,
        in_specs=[any_space] * 9,
        out_specs=(any_space,) * 5,
        scratch_shapes=[
            vmem(precursor.shape, F32),
            vmem(u_star.shape, F32),
            vmem(u_star.shape, F32),
            vmem(u_star.shape, F32),
            vmem(heights.shape, jnp.int32),
            vmem(vert.shape, F32),
            vmem(side.shape, F32),
            vmem(after.shape, F32),
            vmem(span.shape, F32),
            vmem((2 * vert.shape[0], vert.shape[1]), BF16),
            vmem(span.shape, BF16),
            vmem(span.shape, BF16),
            vmem((16, levels), F32),
            vmem((16, levels), F32),
            vmem((16, levels), F32),
            vmem((16, levels), F32),
            vmem((3, rows, levels), F32),
            vmem((3, rows, levels), F32),
            vmem((4, 2 * 128, levels), F32),
            vmem((groups, 2, 128), F32),
            vmem((NZ, NY, 2, 128), F32),
            vmem((groups, 128), F32),
            vmem((32, 128), F32),
            vmem((2, 16, 128), F32),
            vmem((half * rows, 2 * levels), F32),
            vmem((half * rows, 2 * levels), BF16),
            vmem((half * rows, 2 * levels), BF16),
            vmem((2, 2 * levels, half * rows // 2), F32),
            vmem((2, NZ, NY, per, half * rows // 2), F32),
            vmem((half, per, width), F32),
            vmem((per, width), F32),
            vmem((2, per, width), F32),
            vmem((2, per, width), F32),
            vmem((2, per, width), F32),
            vmem((2, per, width), F32),
            vmem(precursor.shape, F32),
            dma((9,)),
            dma((4,)),
            dma((4,)),
            dma((groups,)),
            dma((groups,)),
            dma((2, groups)),
            dma((2, groups)),
            dma((2,)),
            dma((2,)),
            dma((5,)),
            pltpu.SemaphoreType.REGULAR((2,)),
            pltpu.SemaphoreType.REGULAR,
        ],
        compiler_params=pltpu.CompilerParams(
            collective_id=0, has_side_effects=True, vmem_limit_bytes=56 * 2**20
        ),
        name="section",
    )(precursor, u_star, v_star, w_star, heights, vert, side, after, span)
    precursor_next, pressure = pl.pallas_call(
        finish,
        out_shape=(
            jax.ShapeDtypeStruct(precursor.shape, F32),
            jax.ShapeDtypeStruct((2, levels // groups * planes, width), F32),
        ),
        in_specs=[any_space] * 6,
        out_specs=(any_space,) * 2,
        scratch_shapes=[
            vmem((half, per, width), F32),
            vmem((2, per, width), F32),
            vmem((2, per, width), F32),
            vmem((per, width), F32),
            vmem((per, width), F32),
            vmem(precursor.shape, F32),
            vmem((half, per, width), F32),
            vmem((2, width // 128, levels // groups * planes, 128), F32),
            dma((7,)),
            dma((2 * width // 128,)),
        ],
        compiler_params=pltpu.CompilerParams(vmem_limit_bytes=56 * 2**20),
        name="finish",
    )(*held, inv)
    return precursor_next, pressure.reshape(2, levels // groups, planes, width)


def solution(mesh):
    placed = (
        P(None, "gx", "gy", None),
        P("gx", "gy", None),
        P("gx", "gy", None),
        P("gx", "gy", None),
        P("gx", "gy"),
    )
    return jax.shard_map(
        on_device,
        mesh=mesh,
        in_specs=placed,
        out_specs=(P(None, "gx", "gy", None), P(None, "gy", "gx", None)),
        check_vma=False,
    )
```

time: 54.9 us -> 47.9 us (0.87)
  the two profiles are of different devices: /device:TPU:199 before, /device:TPU:8 now
where the time goes in v2:
time: 47.9 us; the launch traced here: 47.7 us
  Pallas kernels  47.1 us (98%)
  between operations  0.64 us (1%)
    pallas_call x1, Pallas kernels, on_device(): pl.pallas_call(kernel, out_shape=between, in_specs=[any_space] * 9, out_s...  44.4 us
    pallas_call x1, Pallas kernels, on_device(): pl.pallas_call(finish, out_shape=(jax.ShapeDtypeStruct(precursor.shape, F...  2.72 us

profile of v2, /device:TPU:8, one launch (start us, length us, event | category | flops | bytes accessed | tf_op | source)
XLA Modules:
  0.0 47.7 jit_solution(14723360634756749835)
XLA Ops:
  0.6 44.4 %section.1 = (f32[3,4,32,128]{3,2,1,0:T(8,128)}, f32[16,8,1024]{2,1,0:T(8,128)}, f32[2,8,1024]{2,1,0:T(8,128)}, f32[2,8,1024]{2,1,0:T(8,128)}, f32[8,1024]{1,0:T(8,128)}) custom-call(f32[3,4,32,128]{3,2,1,0:T(8,128)} %prec_hbm.1, f32[32,32,128]{2,1,0:T(8,128)} %u_hbm.1, f32[32,32,128]{2,1,0:T(8,128)} %v_hbm.1, f32[32,32,128]{2,1,0:T(8,128)} %w_hbm.1, ...), custom_call_target="tpu_custom_call" | custom-call | tf_op jit(solution)/shard_map/section/pallas_call | solution.py:683
  45.0 2.7 %finish.1 = (f32[3,4,32,128]{3,2,1,0:T(8,128)}, f32[2,128,1024]{2,1,0:T(8,128)}) custom-call(f32[3,4,32,128]{3,2,1,0:T(8,128)} %get-tuple-element.9.next_in, f32[16,8,1024]{2,1,0:T(8,128)} %get-tuple-element.10.bands_hbm, f32[2,8,1024]{2,1,0:T(8,128)} %get-tuple-element.11.left_hbm, f32[2,8,1024]{2,1,0:T(8,128)} %get-tuple-element.12.right_hbm, ...), custom_call_target="tpu_custom_call" | custom-call | tf_op jit(solution)/shard_map/finish/pallas_call | solution.py:743

commit v3 on v2

--- a/solution.py
+++ b/solution.py
@@ -93,12 +93,12 @@
 
 def kernel(
     prec_hbm, u_hbm, v_hbm, w_hbm, heights_hbm, vert_hbm, side_hbm, after_hbm, span_hbm,
-    next_hbm, bands_hbm, left_hbm, right_hbm, beyond_hbm,
+    next_v, bands, left_to, right_to, beyond,
     prec, u, v, w, heights, vert_f32, side_f32, after_f32, span_f32, vert, span_hi, span_lo,
     south_out, north_out, south_in, north_in, west_in, east_in,
     spread, side_out, side_in, side_v, side_u, side_rows,
-    rhs, rhs_hi, rhs_lo, outgoing, incoming, bands, beyond, left_out, right_out, left_in, right_in, next_v,
-    load_sem, halo_send, halo_recv, side_send, side_recv, send_sem, recv_sem, edge_send, edge_recv, store_sem, late_in, all_in,
+    rhs, rhs_hi, rhs_lo, outgoing, incoming, left_out, right_out, left_in, right_in,
+    load_sem, halo_send, halo_recv, side_send, side_recv, send_sem, recv_sem, edge_send, edge_recv, late_in, all_in,
 ):
     gx, gy = lax.axis_index("gx"), lax.axis_index("gy")
     count_x, count_y = lax.axis_size("gx"), lax.axis_size("gy")
@@ -258,8 +258,8 @@
         return pltpu.make_async_remote_copy(
             outgoing.at[c, pl.ds(pl.multiple_of(8 * other, 8), 8)],
             incoming.at[c, z, y],
-            send_sem.at[c, other],
-            recv_sem.at[c, z * NY + y],
+            send_sem.at[c],
+            recv_sem.at[c, z],
             device_id={"gy": other},
             device_id_type=MESH,
         )
@@ -268,8 +268,8 @@
         return pltpu.make_async_remote_copy(
             side_out.at[other],
             side_in.at[z, y],
-            side_send.at[other],
-            side_recv.at[z * NY + y],
+            side_send,
+            side_recv.at[z],
             device_id={"gy": other},
             device_id_type=MESH,
         )
@@ -366,45 +366,51 @@
     def _():
         split_tables()
 
+    def same_class():
+        for z in (2, 3):
+
+            @pl.when(my_z == z)
+            def _():
+                pl.semaphore_wait(all_in, 1)
+                send(side_block, z)
+                for c in range(2):
+                    send(functools.partial(block, c), z)
+
+    @pl.when(jnp.logical_and(jnp.logical_not(last), jnp.logical_not(early)))
+    def _():
+        same_class()
+
     for copy in halos:
         copy.wait_recv()
-    for x in (3, 2, 1, 0):
-        a, b, c = prec[0, x], prec[1, x], prec[2, x]
-        for k in range(3):
-            q = prec[k, x]
-            west = west_in[k] if x == 0 else prec[k, x - 1]
-            east = east_in[k] if x == 3 else prec[k, x + 1]
-            place = 4 * k + x
-            south = row_shift(q, south_in[place : place + 1], False)
-            north = row_shift(q, north_in[place : place + 1], True)
-            next_v[k, x] = stencil(q, a, b, c, east, west, north, south)
-    next_store = pltpu.make_async_copy(next_v, next_hbm, store_sem.at[0])
-    next_store.start()
+    def step(k, x):
+        q = prec[k, x]
+        west = west_in[k] if x == 0 else prec[k, x - 1]
+        east = east_in[k] if x == 3 else prec[k, x + 1]
+        place = 4 * k + x
+        south = row_shift(q, south_in[place : place + 1], False)
+        north = row_shift(q, north_in[place : place + 1], True)
+        next_v[k, x] = stencil(q, prec[0, x], prec[1, x], prec[2, x], east, west, north, south)
+
+    step(0, 3)
 
     @pl.when(last)
     def _():
         side(next_v[0, 3])
-        for z in range(NZ):
-
-            @pl.when(jnp.logical_or(early, my_z != z))
-            def _():
-                send(side_block, z)
-
-        for z in range(NZ):
-
-            @pl.when(jnp.logical_or(early, my_z != z))
-            def _():
-                send(functools.partial(block, 1), z)
-
-    for z in (2, 3):
-
-        @pl.when(my_z == z)
-        def _():
-            pl.semaphore_wait(all_in, 1)
-            send(side_block, z)
-            for c in range(2):
-                send(functools.partial(block, c), z)
-
+        for c in range(2):
+            for z in range(NZ):
+
+                @pl.when(jnp.logical_or(early, my_z != z))
+                def _():
+                    send(functools.partial(block, 1) if c else side_block, z)
+
+    @pl.when(jnp.logical_and(last, jnp.logical_not(early)))
+    def _():
+        same_class()
+
+    for k in range(3):
+        for x in range(4):
+            if (k, x) != (0, 3):
+                step(k, x)
     side_u[...] = jnp.zeros_like(side_u)
     side_rows[...] = jnp.zeros_like(side_rows)
 
@@ -446,23 +452,21 @@
                 side_rows[y0, 2 * m + 1 : 2 * m + 2] = found[m][y0 : y0 + 1]
         return jnp.concatenate([side_rows[0], side_rows[1]], 1)
 
-    def arrived(make, z):
-        def one(i, _):
-            other = i * NZ + z
-
-            @pl.when(other != gy)
-            def _():
-                make(other, z, i).wait_recv()
-
-            return 0
-
-        lax.fori_loop(0, NY, one, 0)
+    def arrived(buffer, sem, z):
+        @pl.when(z == my_z)
+        def _():
+            here = buffer.at[pl.ds(0, NY - 1)]
+            pltpu.make_async_copy(here, here, sem).wait()
+
+        @pl.when(z != my_z)
+        def _():
+            pltpu.make_async_copy(buffer, buffer, sem).wait()
 
     def receive(c, step):
         z = step if step < 2 else jnp.where(my_z == 2, 5 - step, step)
         if c == 0:
-            arrived(side_block, z)
-        arrived(functools.partial(block, c), z)
+            arrived(side_in.at[z], side_recv.at[z], z)
+        arrived(incoming.at[c, z], recv_sem.at[c, z], z)
         value = regrouped(c, z)
         if c == 0:
             value = jnp.concatenate([value, sides(z)], 0)
@@ -515,26 +519,17 @@
         for k, x in enumerate(CHUNKS[1]):
             bands[x] = bands[x] + total[8 * k : 8 * k + 8]
 
-    stores = [
-        pltpu.make_async_copy(bands, bands_hbm, store_sem.at[1]),
-        pltpu.make_async_copy(beyond, beyond_hbm, store_sem.at[2]),
-        pltpu.make_async_copy(left_in, left_hbm, store_sem.at[3]),
-        pltpu.make_async_copy(right_in, right_hbm, store_sem.at[4]),
-    ]
-    stores[0].start()
-    stores[1].start()
     to_right.wait_recv()
-    stores[2].start()
+    left_to[...] = left_in[...]
 
     @pl.when(jnp.logical_not(last))
     def _():
         to_left.wait_recv()
+        right_to[...] = right_in[...]
 
     @pl.when(last)
     def _():
-        right_in[...] = jnp.zeros_like(right_in)
-
-    stores[3].start()
+        right_to[...] = jnp.zeros_like(right_to)
 
     for copy in halos:
         copy.wait_send()
@@ -544,50 +539,28 @@
     def _():
         to_left.wait_send()
 
-    def sent(other, _):
-        @pl.when(other != gy)
-        def _():
-            side_block(other, my_z, my_y).wait_send()
-            for c in range(2):
-                block(c, other, my_z, my_y).wait_send()
-
-        return 0
-
-    lax.fori_loop(0, count_y, sent, 0)
-    next_store.wait()
-    for store in stores:
-        store.wait()
+    gone = side_out.at[pl.ds(0, count_y - 1)]
+    pltpu.make_async_copy(gone, gone, side_send).wait()
+    for c in range(2):
+        gone = outgoing.at[c, pl.ds(0, 8 * (count_y - 1))]
+        pltpu.make_async_copy(gone, gone, send_sem.at[c]).wait()
 
 
 def finish(
-    next_in, bands_hbm, left_hbm, right_hbm, beyond_hbm, inv_hbm,
+    next_in, bands, left_in, right_in, beyond, inv_hbm,
     next_hbm, press_hbm,
-    bands, left_in, right_in, beyond, inv, next_v, solved, press_v,
+    inv, solved, press_v,
     load_sem, store_sem,
 ):
     gx, gy = lax.axis_index("gx"), lax.axis_index("gy")
     first, last = gx == 0, gx == lax.axis_size("gx") - 1
     width = inv.shape[1]
     half = bands.shape[0]
-    loads = [
-        pltpu.make_async_copy(source, target, load_sem.at[i])
-        for i, (source, target) in enumerate(
-            (
-                (bands_hbm, bands),
-                (left_hbm, left_in),
-                (right_hbm, right_in),
-                (beyond_hbm, beyond),
-                (inv_hbm.at[gy], inv),
-                (next_in, next_v),
-            )
-        )
-    ]
-    for load in loads:
-        load.start()
-    for load in loads:
-        load.wait()
-    next_store = pltpu.make_async_copy(next_v, next_hbm, load_sem.at[6])
+    load = pltpu.make_async_copy(inv_hbm.at[gy], inv, load_sem.at[0])
+    load.start()
+    next_store = pltpu.make_async_copy(next_in, next_hbm, load_sem.at[1])
     next_store.start()
+    load.wait()
 
     lane = lax.broadcasted_iota(jnp.int32, (8, 128), 1)
     even = lax.broadcasted_iota(jnp.int32, (8, 128), 0) % 2 == 0
@@ -674,17 +647,17 @@
     vmem = pltpu.VMEM
     dma = pltpu.SemaphoreType.DMA
     between = (
-        jax.ShapeDtypeStruct(precursor.shape, F32),
-        jax.ShapeDtypeStruct((half, per, width), F32),
-        jax.ShapeDtypeStruct((2, per, width), F32),
-        jax.ShapeDtypeStruct((2, per, width), F32),
-        jax.ShapeDtypeStruct((per, width), F32),
+        vmem(precursor.shape, F32),
+        vmem((half, per, width), F32),
+        vmem((2, per, width), F32),
+        vmem((2, per, width), F32),
+        vmem((per, width), F32),
     )
     held = pl.pallas_call(
         kernel,
         out_shape=between,
         in_specs=[any_space] * 9,
-        out_specs=(any_space,) * 5,
+        out_specs=(pl.BlockSpec(memory_space=pltpu.VMEM),) * 5,
         scratch_shapes=[
             vmem(precursor.shape, F32),
             vmem(u_star.shape, F32),
@@ -715,23 +688,19 @@
             vmem((half * rows, 2 * levels), BF16),
             vmem((2, 2 * levels, half * rows // 2), F32),
             vmem((2, NZ, NY, per, half * rows // 2), F32),
-            vmem((half, per, width), F32),
-            vmem((per, width), F32),
             vmem((2, per, width), F32),
             vmem((2, per, width), F32),
             vmem((2, per, width), F32),
             vmem((2, per, width), F32),
-            vmem(precursor.shape, F32),
             dma((9,)),
             dma((4,)),
             dma((4,)),
-            dma((groups,)),
-            dma((groups,)),
-            dma((2, groups)),
-            dma((2, groups)),
+            dma,
+            dma((NZ,)),
+            dma((2,)),
+            dma((2, NZ)),
             dma((2,)),
             dma((2,)),
-            dma((5,)),
             pltpu.SemaphoreType.REGULAR((2,)),
             pltpu.SemaphoreType.REGULAR,
         ],
@@ -746,23 +715,18 @@
             jax.ShapeDtypeStruct(precursor.shape, F32),
             jax.ShapeDtypeStruct((2, levels // groups * planes, width), F32),
         ),
-        in_specs=[any_space] * 6,
+        in_specs=[pl.BlockSpec(memory_space=pltpu.VMEM)] * 5 + [any_space],
         out_specs=(any_space,) * 2,
         scratch_shapes=[
-            vmem((half, per, width), F32),
-            vmem((2, per, width), F32),
-            vmem((2, per, width), F32),
             vmem((per, width), F32),
-            vmem((per, width), F32),
-            vmem(precursor.shape, F32),
             vmem((half, per, width), F32),
             vmem((2, width // 128, levels // groups * planes, 128), F32),
-            dma((7,)),
+            dma((2,)),
             dma((2 * width // 128,)),
         ],
-        compiler_params=pltpu.CompilerParams(vmem_limit_bytes=56 * 2**20),
+        compiler_params=pltpu.CompilerParams(vmem_limit_bytes=32 * 2**20),
         name="finish",
-    )(*held, inv)
+    )(*(pltpu.with_memory_space_constraint(value, pltpu.VMEM) for value in held), inv)
     return precursor_next, pressure.reshape(2, levels // groups, planes, width)
 
 

time: 47.9 us -> 44.6 us (0.931)
  Pallas kernels: 47.1 us -> 43.8 us
    pallas_call x1, Pallas kernels: 44.4 us -> 42.2 us  [on_device(): pl.pallas_call(kernel, out_shape=between, in_specs=[any_space] * 9, out_s...]
    pallas_call x1, Pallas kernels: 2.72 us -> 1.57 us  [on_device(): pl.pallas_call(finish, out_shape=(jax.ShapeDtypeStruct(precursor.shape, F...]
where the time goes in v3:
time: 44.6 us; the launch traced here: 44.5 us
  Pallas kernels  43.8 us (98%)
  between operations  0.65 us (1%)
    pallas_call x1, Pallas kernels, on_device(): pl.pallas_call(kernel, out_shape=between, in_specs=[any_space] * 9, out_s...  42.2 us
    pallas_call x1, Pallas kernels, on_device(): pl.pallas_call(finish, out_shape=(jax.ShapeDtypeStruct(precursor.shape, F...  1.57 us

profile of v3, /device:TPU:8, one launch (start us, length us, event | category | flops | bytes accessed | tf_op | source)
XLA Modules:
  0.0 44.5 jit_solution(12425169211212546138)
XLA Ops:
  0.6 0.0 copy-start
  0.6 42.2 %section.1 = (f32[3,4,32,128]{3,2,1,0:T(8,128)S(1)}, f32[16,8,1024]{2,1,0:T(8,128)S(1)}, f32[2,8,1024]{2,1,0:T(8,128)S(1)}, f32[2,8,1024]{2,1,0:T(8,128)S(1)}, f32[8,1024]{1,0:T(8,128)S(1)}) custom-call(f32[3,4,32,128]{3,2,1,0:T(8,128)} %prec_hbm.1, f32[32,32,128]{2,1,0:T(8,128)} %u_hbm.1, f32[32,32,128]{2,1,0:T(8,128)} %v_hbm.1, f32[32,32,128]{2,1,0:T(8,128)} %w_hbm.1, ...), custom_call_target="tpu_custom_call" | custom-call | tf_op jit(solution)/shard_map/section/pallas_call | solution.py:656
  42.9 0.0 copy-done
  42.9 1.6 %finish.1 = (f32[3,4,32,128]{3,2,1,0:T(8,128)}, f32[2,128,1024]{2,1,0:T(8,128)}) custom-call(f32[3,4,32,128]{3,2,1,0:T(8,128)S(1)} %get-tuple-element.9.next_in, f32[16,8,1024]{2,1,0:T(8,128)S(1)} %get-tuple-element.10.bands, f32[2,8,1024]{2,1,0:T(8,128)S(1)} %get-tuple-element.11.left_in, f32[2,8,1024]{2,1,0:T(8,128)S(1)} %get-tuple-element.12.right_in, ...), custom_call_target="tpu_custom_call" | custom-call | tf_op jit(solution)/shard_map/finish/pallas_call | solution.py:712
Async XLA Ops:
  0.6 42.3 %copy-start = (f32[32,8,1024]{2,1,0:T(8,128)S(1)}, f32[32,8,1024]{2,1,0:T(8,128)}, u32[]{:S(2)}) copy-start(f32[32,8,1024]{2,1,0:T(8,128)} %constant.14.clone.inv_hbm) | copy-start | bytes 3145732

commit v4 on v3

--- a/solution.py
+++ b/solution.py
@@ -360,7 +360,12 @@
 
     @pl.when(my_z != 3)
     def _():
-        send_all(3)
+        send_side(3)
+        send(functools.partial(block, 0), 3)
+
+    @pl.when(my_z == 2)
+    def _():
+        send_middle(3)
 
     @pl.when(jnp.logical_not(early))
     def _():
@@ -399,7 +404,7 @@
         for c in range(2):
             for z in range(NZ):
 
-                @pl.when(jnp.logical_or(early, my_z != z))
+                @pl.when(jnp.logical_and(jnp.logical_or(early, my_z != z), jnp.logical_not(early) if c * z == 3 else True))
                 def _():
                     send(functools.partial(block, 1) if c else side_block, z)
 
@@ -513,6 +518,10 @@
     @pl.when(jnp.logical_not(first))
     def _():
         to_left.start()
+
+    @pl.when(early)
+    def _():
+        send(functools.partial(block, 1), 3)
 
     for step in range(NZ):
         total = receive(1, step)

time: 44.6 us -> 44.6 us (level)
  no operation moved by 1% of the time
where the time goes in v4:
time: 44.6 us; the launch traced here: 44.5 us
  Pallas kernels  43.9 us (98%)
  between operations  0.65 us (1%)
    pallas_call x1, Pallas kernels, on_device(): pl.pallas_call(kernel, out_shape=between, in_specs=[any_space] * 9, out_s...  42.3 us
    pallas_call x1, Pallas kernels, on_device(): pl.pallas_call(finish, out_shape=(jax.ShapeDtypeStruct(precursor.shape, F...  1.57 us

profile of v4, /device:TPU:8, one launch (start us, length us, event | category | flops | bytes accessed | tf_op | source)
XLA Modules:
  0.0 44.5 jit_solution(16815294781383263010)
XLA Ops:
  0.6 0.0 copy-start
  0.6 42.3 %section.1 = (f32[3,4,32,128]{3,2,1,0:T(8,128)S(1)}, f32[16,8,1024]{2,1,0:T(8,128)S(1)}, f32[2,8,1024]{2,1,0:T(8,128)S(1)}, f32[2,8,1024]{2,1,0:T(8,128)S(1)}, f32[8,1024]{1,0:T(8,128)S(1)}) custom-call(f32[3,4,32,128]{3,2,1,0:T(8,128)} %prec_hbm.1, f32[32,32,128]{2,1,0:T(8,128)} %u_hbm.1, f32[32,32,128]{2,1,0:T(8,128)} %v_hbm.1, f32[32,32,128]{2,1,0:T(8,128)} %w_hbm.1, ...), custom_call_target="tpu_custom_call" | custom-call | tf_op jit(solution)/shard_map/section/pallas_call | solution.py:665
  42.9 0.0 copy-done
  42.9 1.6 %finish.1 = (f32[3,4,32,128]{3,2,1,0:T(8,128)}, f32[2,128,1024]{2,1,0:T(8,128)}) custom-call(f32[3,4,32,128]{3,2,1,0:T(8,128)S(1)} %get-tuple-element.9.next_in, f32[16,8,1024]{2,1,0:T(8,128)S(1)} %get-tuple-element.10.bands, f32[2,8,1024]{2,1,0:T(8,128)S(1)} %get-tuple-element.11.left_in, f32[2,8,1024]{2,1,0:T(8,128)S(1)} %get-tuple-element.12.right_in, ...), custom_call_target="tpu_custom_call" | custom-call | tf_op jit(solution)/shard_map/finish/pallas_call | solution.py:721
Async XLA Ops:
  0.6 42.3 %copy-start = (f32[32,8,1024]{2,1,0:T(8,128)S(1)}, f32[32,8,1024]{2,1,0:T(8,128)}, u32[]{:S(2)}) copy-start(f32[32,8,1024]{2,1,0:T(8,128)} %constant.14.clone.inv_hbm) | copy-start | bytes 3145732
